TPU v7x, 32 devices: a whole 2x2x4 slice. The times are simulated.
32 devices in a mesh: section: 2 (over core), seq: 4 (over z), cfg: 4 (over y, x).
Axes of the slice: x: 2, y: 2, z: 4, core: 2. Of those that a mesh axis runs over, the one named last changes fastest.
Arguments:
- hidden_states: bfloat16 [4, 4, 64, 3072], P('cfg', None, 'seq'), may hold values from -250 to 250
- latent: float32 [2, 4, 64, 64], P('section', None, 'seq'), may hold values from -6 to 6
- stale_cache: bfloat16 [2, 4, 4, 256, 128], P('section', 'cfg', 'seq'), may hold values from -140 to 140
- qkv_weight: bfloat16 [2, 3072, 3, 256], P('section', None, None, 'cfg'), may hold values from -0.109375 to 0.109375
- out_weight: bfloat16 [2, 3072, 256], P('section', 'seq', 'cfg'), may hold values from -0.375 to 0.375
- modulation: float32 [2, 6, 3072], P('section'), may hold values from -2.5 to 2.5
- out_modulation: float32 [2, 3072], replicated, may hold values from -2.5 to 2.5
- proj_weight: bfloat16 [3072, 64], replicated, may hold values from -0.109375 to 0.109375
- solver_coef: float32 [2, 3], P('section'), may hold values from 0.5 to 2
- video_len: int32 [2], replicated, may hold values from 15 to 30, as said below
- text_len: int32 [4], replicated, may hold values from 1 to 226, as said below
- positions: int32 [3, 2, 4, 64], P(None, None, None, 'seq'), may hold values from 0 to 47
Outputs:
- new_latent: float32 [2, 4, 64, 64], P('section', None, 'seq')
- new_cache: bfloat16 [2, 4, 4, 256, 128], P('section', 'cfg', 'seq')
Inputs may be any that keep to these rules, and one draw needn't show every extreme that they name: `video_len`: in every draw one request has exactly 30 video tokens. `text_len`: in every draw some sequence has all 226 text tokens live.
All inputs are finite; a program needn't handle non-finite values.
Results may differ from a plain program's by a relative error of at most 0.02.
Values may be sent and summed in bfloat16 or wider, within the bound.
A program may use at most 128 MiB of HBM per device.

v0:
```python
import math

import jax
import jax.numpy as jnp
from jax import lax
from jax.sharding import PartitionSpec as P

HD = 64
TEXT = 226


def from_behind(value, axis, steps):
    count = lax.axis_size(axis)
    pairs = [(source, (source + steps) % count) for source in range(count)]
    return lax.ppermute(value, axis, pairs)


def row_norm(values):
    centered = values - jnp.mean(values, axis=-1, keepdims=True)
    return centered * lax.rsqrt(jnp.mean(centered * centered, axis=-1, keepdims=True) + 1e-05)


def head_norm(values):
    centered = values - jnp.mean(values, axis=-1, keepdims=True)
    return centered * lax.rsqrt(jnp.mean(centered * centered, axis=-1, keepdims=True) + 1e-06)


def rope_angles(places, head_size):
    half_size = head_size // 2
    pairs_t = head_size // 8
    pairs_h = (half_size - pairs_t) // 2
    pair_index = jnp.arange(half_size)
    first_part = pair_index < pairs_t
    second_part = jnp.logical_and(pair_index >= pairs_t, pair_index < pairs_t + pairs_h)
    third_part = pair_index >= pairs_t + pairs_h
    local_index = jnp.where(
        first_part,
        pair_index,
        jnp.where(second_part, pair_index - pairs_t, pair_index - pairs_t - pairs_h),
    )
    axis_span = jnp.where(first_part, 2 * pairs_t, 2 * pairs_h)
    frequency = jnp.exp(
        -math.log(10000.0) * 2.0 * local_index.astype(jnp.float32) / axis_span.astype(jnp.float32)
    )
    angles = places[0][..., None] * first_part.astype(jnp.float32)
    angles = angles + places[1][..., None] * second_part.astype(jnp.float32)
    angles = angles + places[2][..., None] * third_part.astype(jnp.float32)
    return angles * frequency


def rotate(values, cos_table, sin_table):
    half_size = values.shape[-1] // 2
    first_half = values[..., :half_size]
    second_half = values[..., half_size:]
    return jnp.concatenate(
        [
            first_half * cos_table - second_half * sin_table,
            second_half * cos_table + first_half * sin_table,
        ],
        axis=-1,
    )


def spread(values):
    return lax.all_gather(values, "cfg", axis=0, tiled=True)


def handoff(values):
    return from_behind(values, "section", 1)


def per_device(
    hidden_states,
    latent,
    stale_cache,
    qkv_weight,
    out_weight,
    modulation,
    out_modulation,
    proj_weight,
    solver_coef,
    video_len,
    text_len,
    positions,
):
    section_id = lax.axis_index("section")
    shard_id = lax.axis_index("seq")
    seq_devices = lax.axis_size("seq")
    patches = hidden_states.shape[1]
    patch_dev = hidden_states.shape[2]
    width = hidden_states.shape[3]
    patch_len = patch_dev * seq_devices
    total_len = patch_len * patches
    group_heads = qkv_weight.shape[3] // HD
    qkv_full = qkv_weight[0].reshape(width, 3, group_heads, HD)
    out_full = lax.all_gather(out_weight[0], "seq", axis=0, tiled=True).reshape(
        width, group_heads, HD
    )
    mod_rows = modulation[0]
    stale_rows = stale_cache[0, 0, 0]
    my_sequence = shard_id // group_heads
    row_ids = jnp.arange(total_len)
    text_limit = lax.dynamic_index_in_dim(text_len, my_sequence, keepdims=False)
    video_limit = lax.dynamic_index_in_dim(video_len, my_sequence // 2, keepdims=False)
    live_keys = jnp.where(row_ids < TEXT, row_ids < text_limit, row_ids - TEXT < video_limit)
    key_patch = row_ids // patch_len
    query_block = patch_len
    while query_block > 1024 and query_block % 2 == 0:
        query_block = query_block // 2
    scale_factor = HD ** (-0.5)
    key_cache = stale_rows
    received = jnp.zeros_like(hidden_states[:, :1])
    pieces = []
    for tick_id in range(patches + 1):
        first_patch = jnp.clip(tick_id - section_id, 0, patches - 1)
        source = hidden_states[:, min(tick_id, patches - 1)][:, None]
        hidden = jnp.where(section_id == 0, source, received)
        run_key_cache = key_cache
        patch_count = hidden.shape[1]
        row_place = (
            (first_patch + jnp.arange(patch_count))[:, None] * patch_len
            + shard_id * patch_dev
            + jnp.arange(patch_dev)[None, :]
        )
        text_rows = (row_place < TEXT)[:, :, None]
        run_normed = row_norm(hidden.astype(jnp.float32))
        shift_rows = jnp.where(text_rows, mod_rows[3], mod_rows[0])
        scale_rows = jnp.where(text_rows, mod_rows[4], mod_rows[1])
        gate_rows = jnp.where(text_rows, mod_rows[5], mod_rows[2])
        mixed_rows = (run_normed * (1.0 + scale_rows) + shift_rows).astype(jnp.bfloat16)
        mixed_rows = spread(mixed_rows)
        seq_count = mixed_rows.shape[0]
        projected = jnp.einsum(
            "spqd,djge->sgjpqe", mixed_rows, qkv_full, preferred_element_type=jnp.float32
        )
        places = lax.dynamic_slice_in_dim(positions, first_patch, patch_count, 2).astype(
            jnp.float32
        )
        angles = rope_angles(places, HD)
        angles = jnp.where(text_rows[None], 0.0, angles)
        angles = jnp.repeat(angles, 2, axis=0)[:, None]
        cos_table = jnp.cos(angles)
        sin_table = jnp.sin(angles)
        queries = rotate(head_norm(projected[:, :, 0]), cos_table, sin_table)
        key_part = rotate(head_norm(projected[:, :, 1]), cos_table, sin_table)
        stacked = jnp.stack([queries, key_part, projected[:, :, 2]], axis=2).astype(jnp.bfloat16)
        outgoing = stacked.reshape(seq_count * group_heads, 3, patch_count, patch_dev * HD)
        incoming = lax.all_to_all(outgoing, "seq", split_axis=0, concat_axis=3, tiled=True)
        incoming = incoming.reshape(3, patch_count * patch_len, HD)
        fresh_rows = jnp.concatenate([incoming[1], incoming[2]], axis=-1)
        run_key_cache = lax.dynamic_update_slice_in_dim(
            run_key_cache, fresh_rows, first_patch * patch_len, 0
        )
        block_count = patch_count * patch_len // query_block

        def attend(work_item):
            query_rows, block_id = work_item
            patch_now = first_patch + block_id * query_block // patch_len
            key_rows = jnp.where((key_patch <= patch_now)[:, None], run_key_cache, stale_rows)
            scores = (
                jnp.dot(query_rows, key_rows[:, :HD].T, preferred_element_type=jnp.float32)
                * scale_factor
            )
            scores = jnp.where(live_keys[None, :], scores, -jnp.inf)
            row_max = jnp.max(scores, axis=1, keepdims=True)
            weights = jnp.exp(scores - row_max)
            row_sum = jnp.sum(weights, axis=1, keepdims=True)
            combined = jnp.dot(
                weights.astype(jnp.bfloat16), key_rows[:, HD:], preferred_element_type=jnp.float32
            )
            return (combined / row_sum).astype(jnp.bfloat16)

        attended = lax.map(
            attend, (incoming[0].reshape(block_count, query_block, HD), jnp.arange(block_count))
        )
        attended = attended.reshape(patch_count, seq_devices, patch_dev * HD)[None]
        returned = lax.all_to_all(attended, "seq", split_axis=2, concat_axis=0, tiled=True)
        returned = returned.reshape(seq_count, group_heads, patch_count, patch_dev, HD)
        update = lax.psum_scatter(
            jnp.einsum("sgpqe,dge->spqd", returned, out_full, preferred_element_type=jnp.float32),
            "cfg",
            scatter_dimension=0,
            tiled=True,
        )
        result = (hidden.astype(jnp.float32) + gate_rows * update).astype(jnp.bfloat16)
        result, key_cache = (result, run_key_cache)
        received = handoff(result)
        if tick_id > 0:
            final_rows = jnp.where(section_id == 1, result, received)
            normed = row_norm(final_rows.astype(jnp.float32))
            normed_out = (normed * (1.0 + out_modulation[1]) + out_modulation[0]).astype(
                jnp.bfloat16
            )
            own_values = jnp.einsum(
                "sqd,do->sqo", normed_out[:, 0], proj_weight, preferred_element_type=jnp.float32
            )
            all_values = lax.all_gather(own_values, "cfg", axis=0, tiled=True)
            predicted = lax.dynamic_slice_in_dim(all_values, 2 * section_id, 2, 0)
            solver_row = solver_coef[0]
            guided = predicted[0] + solver_row[2] * (predicted[1] - predicted[0])
            pieces.append(solver_row[0] * latent[0, tick_id - 1] + solver_row[1] * guided)
    new_latent = jnp.stack(pieces, axis=0)[None]
    return (new_latent, key_cache[None, None, None])


def solution(mesh):
    return jax.shard_map(
        per_device,
        mesh=mesh,
        in_specs=(
            P("cfg", None, "seq", None),
            P("section", None, "seq", None),
            P("section", "cfg", "seq", None, None),
            P("section", None, None, "cfg"),
            P("section", "seq", "cfg"),
            P("section", None, None),
            P(),
            P(),
            P("section", None),
            P(),
            P(),
            P(None, None, None, "seq"),
        ),
        out_specs=(P("section", None, "seq", None), P("section", "cfg", "seq", None, None)),
        check_vma=False,
    )
```

profile of v0, /device:TPU:0, one launch (start us, length us, event | category | flops | bytes accessed | tf_op | source)
XLA Modules:
  0.0 351.9 jit_solution(4757130300340748753)
XLA Ops:
  11.3 11.0 %all_gather.30 = bf16[4,1,16,3072]{3,2,1,0:T(8,128)(2,1)S(1)} all-gather(bf16[1,1,16,3072]{3,2,1,0:T(8,128)(2,1)S(1)} %fusion.82), channel_id=1, replica_groups=mesh['section'=2,'seq'=4,'cfg'=4] {'cfg'}, dimensions={0}, use_global_device_ids=true | all-gather | bytes 491520 | tf_op jit(solution)/shard_map/all_gather | solution.py:65
  25.0 4.9 %all-to-all-start = ((bf16[4,3,1,1024]{3,1,2,0:T(4,128)(2,1)}), bf16[4,3,1,1024]{3,1,2,0:T(4,128)(2,1)S(1)}, u32[]{:S(2)}, u32[]{:S(2)}) async-start(bf16[4,3,1,1024]{3,1,2,0:T(4,128)(2,1)} %pad_maximum_fusion), calls=%async_computation | async-start | bytes 65536 | tf_op jit(solution)/shard_map/all_to_all | solution.py:148
  32.5 3.0 all-to-all-done
  38.7 3.2 all-to-all-start.1
  42.1 15.7 %all-gather = bf16[1,3072,64]{1,2,0:T(8,128)(2,1)S(1)} all-gather(bf16[1,768,64]{1,2,0:T(8,128)(2,1)S(1)} %copy-done.4), channel_id=2, replica_groups=mesh['section'=2,'seq'=4,'cfg'=4] {'seq'}, dimensions={1}, use_global_device_ids=true | all-gather | bytes 491520 | tf_op jit(solution)/shard_map/all_gather | solution.py:96
  59.2 25.7 %reduce-scatter.21.cloned.1.call-done = f32[1,1,16,3072]{3,2,0,1:T(8,128)} async-done(((f32[4,1,16,3072]{3,2,0,1:T(8,128)}), f32[1,1,16,3072]{3,2,0,1:T(8,128)}) %reduce-scatter.21.cloned.1.call-update) | async-done | bytes 196624
  87.8 9.4 %all_gather.32 = bf16[4,1,16,3072]{3,2,1,0:T(8,128)(2,1)S(1)} all-gather(bf16[1,1,16,3072]{3,2,1,0:T(8,128)(2,1)S(1)} %fusion.78), channel_id=1, replica_groups=mesh['section'=2,'seq'=4,'cfg'=4] {'cfg'}, dimensions={0}, use_global_device_ids=true | all-gather | bytes 491520 | tf_op jit(solution)/shard_map/all_gather | solution.py:65
  99.6 4.6 %all-to-all-start.2 = ((bf16[4,3,1,1024]{3,1,2,0:T(4,128)(2,1)}), bf16[4,3,1,1024]{3,1,2,0:T(4,128)(2,1)S(1)}, u32[]{:S(2)}, u32[]{:S(2)}) async-start(bf16[4,3,1,1024]{3,1,2,0:T(4,128)(2,1)} %pad_maximum_fusion.1), calls=%async_computation.2 | async-start | bytes 65536 | tf_op jit(solution)/shard_map/all_to_all | solution.py:148
  104.2 5.6 %all-to-all-done.2 = bf16[4,3,1,1024]{3,1,2,0:T(4,128)(2,1)S(1)} async-done(((bf16[4,3,1,1024]{3,1,2,0:T(4,128)(2,1)}), bf16[4,3,1,1024]{3,1,2,0:T(4,128)(2,1)S(1)}, u32[]{:S(2)}, u32[]{:S(2)}) %all-to-all-start.2) | async-done | bytes 24608 | tf_op jit(solution)/shard_map/all_to_all | solution.py:148
  111.8 7.9 %all_to_all.120 = bf16[4,2,512]{2,1,0:T(2,128)(2,1)S(1)} all-to-all(bf16[4,2,512]{2,1,0:T(2,128)(2,1)S(1)} %reshape.2981), channel_id=1, replica_groups=mesh['section'=2,'seq'=4,'cfg'=4] {'seq'}, dimensions={0} | all-to-all | bytes 16384 | tf_op jit(solution)/shard_map/all_to_all | solution.py:177
  121.1 23.6 %reduce-scatter.23.cloned.1.call-done = f32[1,1,16,3072]{3,2,0,1:T(8,128)} async-done(((f32[4,1,16,3072]{3,2,0,1:T(8,128)}), f32[1,1,16,3072]{3,2,0,1:T(8,128)}) %reduce-scatter.23.cloned.1.call-update) | async-done | bytes 196624
  147.6 9.4 %all_gather.34 = bf16[4,1,16,3072]{3,2,1,0:T(8,128)(2,1)S(1)} all-gather(bf16[1,1,16,3072]{3,2,1,0:T(8,128)(2,1)S(1)} %fusion.74), channel_id=1, replica_groups=mesh['section'=2,'seq'=4,'cfg'=4] {'cfg'}, dimensions={0}, use_global_device_ids=true | all-gather | bytes 491520 | tf_op jit(solution)/shard_map/all_gather | solution.py:65
  159.4 4.6 %all-to-all-start.4 = ((bf16[4,3,1,1024]{3,1,2,0:T(4,128)(2,1)}), bf16[4,3,1,1024]{3,1,2,0:T(4,128)(2,1)S(1)}, u32[]{:S(2)}, u32[]{:S(2)}) async-start(bf16[4,3,1,1024]{3,1,2,0:T(4,128)(2,1)} %pad_maximum_fusion.2), calls=%async_computation.4 | async-start | bytes 65536 | tf_op jit(solution)/shard_map/all_to_all | solution.py:148
  164.0 5.7 %all-to-all-done.4 = bf16[4,3,1,1024]{3,1,2,0:T(4,128)(2,1)S(1)} async-done(((bf16[4,3,1,1024]{3,1,2,0:T(4,128)(2,1)}), bf16[4,3,1,1024]{3,1,2,0:T(4,128)(2,1)S(1)}, u32[]{:S(2)}, u32[]{:S(2)}) %all-to-all-start.4) | async-done | bytes 24608 | tf_op jit(solution)/shard_map/all_to_all | solution.py:148
  171.6 7.9 %all_to_all.121 = bf16[4,2,512]{2,1,0:T(2,128)(2,1)S(1)} all-to-all(bf16[4,2,512]{2,1,0:T(2,128)(2,1)S(1)} %reshape.2983), channel_id=1, replica_groups=mesh['section'=2,'seq'=4,'cfg'=4] {'seq'}, dimensions={0} | all-to-all | bytes 16384 | tf_op jit(solution)/shard_map/all_to_all | solution.py:177
  180.9 23.5 %reduce-scatter.25.cloned.1.call-done = f32[1,1,16,3072]{3,2,0,1:T(8,128)} async-done(((f32[4,1,16,3072]{3,2,0,1:T(8,128)}), f32[1,1,16,3072]{3,2,0,1:T(8,128)}) %reduce-scatter.25.cloned.1.call-update) | async-done | bytes 196624
  207.4 9.5 %all_gather.36 = bf16[4,1,16,3072]{3,2,1,0:T(8,128)(2,1)S(1)} all-gather(bf16[1,1,16,3072]{3,2,1,0:T(8,128)(2,1)S(1)} %fusion.70), channel_id=1, replica_groups=mesh['section'=2,'seq'=4,'cfg'=4] {'cfg'}, dimensions={0}, use_global_device_ids=true | all-gather | bytes 491520 | tf_op jit(solution)/shard_map/all_gather | solution.py:65
  219.2 4.6 %all-to-all-start.6 = ((bf16[4,3,1,1024]{3,1,2,0:T(4,128)(2,1)}), bf16[4,3,1,1024]{3,1,2,0:T(4,128)(2,1)S(1)}, u32[]{:S(2)}, u32[]{:S(2)}) async-start(bf16[4,3,1,1024]{3,1,2,0:T(4,128)(2,1)} %pad_maximum_fusion.3), calls=%async_computation.6 | async-start | bytes 65536 | tf_op jit(solution)/shard_map/all_to_all | solution.py:148
  223.8 5.6 %all-to-all-done.6 = bf16[4,3,1,1024]{3,1,2,0:T(4,128)(2,1)S(1)} async-done(((bf16[4,3,1,1024]{3,1,2,0:T(4,128)(2,1)}), bf16[4,3,1,1024]{3,1,2,0:T(4,128)(2,1)S(1)}, u32[]{:S(2)}, u32[]{:S(2)}) %all-to-all-start.6) | async-done | bytes 24608 | tf_op jit(solution)/shard_map/all_to_all | solution.py:148
  231.5 7.9 %all_to_all.122 = bf16[4,2,512]{2,1,0:T(2,128)(2,1)S(1)} all-to-all(bf16[4,2,512]{2,1,0:T(2,128)(2,1)S(1)} %reshape.2985), channel_id=1, replica_groups=mesh['section'=2,'seq'=4,'cfg'=4] {'seq'}, dimensions={0} | all-to-all | bytes 16384 | tf_op jit(solution)/shard_map/all_to_all | solution.py:177
  241.4 22.8 %reduce-scatter.27.cloned.1.call-done = f32[1,1,16,3072]{3,2,0,1:T(8,128)} async-done(((f32[4,1,16,3072]{3,2,0,1:T(8,128)}), f32[1,1,16,3072]{3,2,0,1:T(8,128)}) %reduce-scatter.27.cloned.1.call-update) | async-done | bytes 196624
  267.2 9.4 %all_gather.38 = bf16[4,1,16,3072]{3,2,1,0:T(8,128)(2,1)S(1)} all-gather(bf16[1,1,16,3072]{3,2,1,0:T(8,128)(2,1)S(1)} %fusion.66), channel_id=1, replica_groups=mesh['section'=2,'seq'=4,'cfg'=4] {'cfg'}, dimensions={0}, use_global_device_ids=true | all-gather | bytes 491520 | tf_op jit(solution)/shard_map/all_gather | solution.py:65
  279.0 4.6 %all-to-all-start.8 = ((bf16[4,3,1,1024]{3,1,2,0:T(4,128)(2,1)}), bf16[4,3,1,1024]{3,1,2,0:T(4,128)(2,1)S(1)}, u32[]{:S(2)}, u32[]{:S(2)}) async-start(bf16[4,3,1,1024]{3,1,2,0:T(4,128)(2,1)} %pad_maximum_fusion.4), calls=%async_computation.8 | async-start | bytes 65536 | tf_op jit(solution)/shard_map/all_to_all | solution.py:148
  283.8 5.4 %all-to-all-done.8 = bf16[4,3,1,1024]{3,1,2,0:T(4,128)(2,1)S(1)} async-done(((bf16[4,3,1,1024]{3,1,2,0:T(4,128)(2,1)}), bf16[4,3,1,1024]{3,1,2,0:T(4,128)(2,1)S(1)}, u32[]{:S(2)}, u32[]{:S(2)}) %all-to-all-start.8) | async-done | bytes 24608 | tf_op jit(solution)/shard_map/all_to_all | solution.py:148
  291.9 3.2 all-to-all-start.9
  295.2 5.5 %all-to-all-done.9 = bf16[4,2,512]{2,1,0:T(2,128)(2,1)S(1)} async-done(((bf16[4,2,512]{2,1,0:T(2,128)(2,1)}), bf16[4,2,512]{2,1,0:T(2,128)(2,1)S(1)}, u32[]{:S(2)}, u32[]{:S(2)}) %all-to-all-start.9) | async-done | bytes 8224 | tf_op jit(solution)/shard_map/all_to_all | solution.py:177
  302.3 7.3 %all-gather.1 = f32[64,64]{1,0:T(8,128)S(1)} all-gather(f32[16,64]{1,0:T(8,128)S(1)} %fusion.105), channel_id=3, replica_groups=mesh['section'=2,'seq'=4,'cfg'=4] {'cfg'}, dimensions={0}, use_global_device_ids=true | all-gather | bytes 20480 | tf_op jit(solution)/shard_map/all_gather | solution.py:197
  310.0 8.2 %all-gather.2 = f32[64,64]{1,0:T(8,128)S(1)} all-gather(f32[16,64]{1,0:T(8,128)S(1)} %fusion.108), channel_id=4, replica_groups=mesh['section'=2,'seq'=4,'cfg'=4] {'cfg'}, dimensions={0}, use_global_device_ids=true | all-gather | bytes 20480 | tf_op jit(solution)/shard_map/all_gather | solution.py:197
  318.5 7.1 %reduce-scatter.29.cloned.1.call-done = f32[1,1,16,3072]{3,2,0,1:T(8,128)} async-done(((f32[4,1,16,3072]{3,2,0,1:T(8,128)}), f32[1,1,16,3072]{3,2,0,1:T(8,128)}) %reduce-scatter.29.cloned.1.call-update) | async-done | bytes 196624
  326.9 8.1 %all-gather.3 = f32[64,64]{1,0:T(8,128)S(1)} all-gather(f32[16,64]{1,0:T(8,128)S(1)} %fusion.111), channel_id=5, replica_groups=mesh['section'=2,'seq'=4,'cfg'=4] {'cfg'}, dimensions={0}, use_global_device_ids=true | all-gather | bytes 20480 | tf_op jit(solution)/shard_map/all_gather | solution.py:197
  335.7 7.2 %all-gather.4 = f32[64,64]{1,0:T(8,128)S(1)} all-gather(f32[16,64]{1,0:T(8,128)S(1)} %fusion.114), channel_id=6, replica_groups=mesh['section'=2,'seq'=4,'cfg'=4] {'cfg'}, dimensions={0}, use_global_device_ids=true | all-gather | bytes 20480 | tf_op jit(solution)/shard_map/all_gather | solution.py:197
  342.9 1.8 fusion.197
  (296 shorter events, 52.8 us)
Async XLA Ops:
  7.2 15.1 %copy-start = (bf16[1,3072,3,64]{1,3,2,0:T(8,128)(2,1)S(1)}, bf16[1,3072,3,64]{1,3,2,0:T(8,128)(2,1)}, u32[]{:S(2)}) copy-start(bf16[1,3072,3,64]{1,3,2,0:T(8,128)(2,1)} %param.15) | copy-start | bytes 3538948
  11.3 11.9 %copy-start.7 = (s32[3,2,4,16]{3,2,1,0:T(4,128)S(1)}, s32[3,2,4,16]{3,2,1,0:T(4,128)}, u32[]{:S(2)}) copy-start(s32[3,2,4,16]{3,2,1,0:T(4,128)} %param.23) | copy-start | bytes 4612
  22.3 7.6 %copy-start.10 = (s32[2]{0:T(128)S(1)}, s32[2]{0:T(128)}, u32[]{:S(2)}) copy-start(s32[2]{0:T(128)} %param.21) | copy-start | bytes 28
  22.3 8.2 %copy-start.11 = (s32[4]{0:T(128)S(1)}, s32[4]{0:T(128)}, u32[]{:S(2)}) copy-start(s32[4]{0:T(128)} %param.22) | copy-start | bytes 52
  22.3 10.2 %copy-start.1 = (bf16[1,1,1,256,128]{4,3,2,1,0:T(8,128)(2,1)S(1)}, bf16[1,1,1,256,128]{4,3,2,1,0:T(8,128)(2,1)}, u32[]{:S(2)}) copy-start(bf16[1,1,1,256,128]{4,3,2,1,0:T(8,128)(2,1)} %param.14) | copy-start | bytes 196612
  23.1 18.9 %copy-start.4 = (bf16[1,768,64]{1,2,0:T(8,128)(2,1)S(1)}, bf16[1,768,64]{1,2,0:T(8,128)(2,1)}, u32[]{:S(2)}) copy-start(bf16[1,768,64]{1,2,0:T(8,128)(2,1)} %param.16) | copy-start | bytes 294916
  25.0 10.5 %all-to-all-start = ((bf16[4,3,1,1024]{3,1,2,0:T(4,128)(2,1)}), bf16[4,3,1,1024]{3,1,2,0:T(4,128)(2,1)S(1)}, u32[]{:S(2)}, u32[]{:S(2)}) async-start(bf16[4,3,1,1024]{3,1,2,0:T(4,128)(2,1)} %pad_maximum_fusion), calls=%async_computation | async-start | bytes 65536 | tf_op jit(solution)/shard_map/all_to_all | solution.py:148
  38.7 19.1 %all-to-all-start.1 = ((bf16[4,2,512]{2,1,0:T(2,128)(2,1)}), bf16[4,2,512]{2,1,0:T(2,128)(2,1)S(1)}, u32[]{:S(2)}, u32[]{:S(2)}) async-start(bf16[4,2,512]{2,1,0:T(2,128)(2,1)} %reshape.2979), calls=%async_computation.1 | async-start | bytes 16384 | tf_op jit(solution)/shard_map/all_to_all | solution.py:177
  42.0 42.9 %copy-start.3 = (bf16[1,4,16,3072]{3,2,1,0:T(8,128)(2,1)S(1)}, bf16[1,4,16,3072]{3,2,1,0:T(8,128)(2,1)}, u32[]{:S(2)}) copy-start(bf16[1,4,16,3072]{3,2,1,0:T(8,128)(2,1)} %param.12) | copy-start | bytes 1179652
  42.0 42.9 %reduce-scatter.21.cloned.1.call-start = ((), (), s32[]{:S(2)}) async-start(), calls=%async_computation.15 | async-start | bytes 983040
  85.9 1.4 collective-permute-start
  99.6 10.2 %all-to-all-start.2 = ((bf16[4,3,1,1024]{3,1,2,0:T(4,128)(2,1)}), bf16[4,3,1,1024]{3,1,2,0:T(4,128)(2,1)S(1)}, u32[]{:S(2)}, u32[]{:S(2)}) async-start(bf16[4,3,1,1024]{3,1,2,0:T(4,128)(2,1)} %pad_maximum_fusion.1), calls=%async_computation.2 | async-start | bytes 65536 | tf_op jit(solution)/shard_map/all_to_all | solution.py:148
  104.2 40.5 %reduce-scatter.23.cloned.1.call-start = ((), (), s32[]{:S(2)}) async-start(), calls=%async_computation.16 | async-start | bytes 983040
  145.7 1.4 collective-permute-start.1
  159.4 10.3 %all-to-all-start.4 = ((bf16[4,3,1,1024]{3,1,2,0:T(4,128)(2,1)}), bf16[4,3,1,1024]{3,1,2,0:T(4,128)(2,1)S(1)}, u32[]{:S(2)}, u32[]{:S(2)}) async-start(bf16[4,3,1,1024]{3,1,2,0:T(4,128)(2,1)} %pad_maximum_fusion.2), calls=%async_computation.4 | async-start | bytes 65536 | tf_op jit(solution)/shard_map/all_to_all | solution.py:148
  164.0 40.5 %reduce-scatter.25.cloned.1.call-start = ((), (), s32[]{:S(2)}) async-start(), calls=%async_computation.17 | async-start | bytes 983040
  205.4 1.4 collective-permute-start.2
  219.2 10.2 %all-to-all-start.6 = ((bf16[4,3,1,1024]{3,1,2,0:T(4,128)(2,1)}), bf16[4,3,1,1024]{3,1,2,0:T(4,128)(2,1)S(1)}, u32[]{:S(2)}, u32[]{:S(2)}) async-start(bf16[4,3,1,1024]{3,1,2,0:T(4,128)(2,1)} %pad_maximum_fusion.3), calls=%async_computation.6 | async-start | bytes 65536 | tf_op jit(solution)/shard_map/all_to_all | solution.py:148
  223.8 40.5 %reduce-scatter.27.cloned.1.call-start = ((), (), s32[]{:S(2)}) async-start(), calls=%async_computation.18 | async-start | bytes 983040
  230.4 10.3 %copy-start.8 = (f32[1,3]{1,0:T(1,128)S(1)}, f32[1,3]{1,0:T(1,128)}, u32[]{:S(2)}) copy-start(f32[1,3]{1,0:T(1,128)} %param.20) | copy-start | bytes 40
  230.4 11.0 %copy-start.6 = (f32[2,3072]{1,0:T(2,128)S(1)}, f32[2,3072]{1,0:T(2,128)}, u32[]{:S(2)}) copy-start(f32[2,3072]{1,0:T(2,128)} %param.18) | copy-start | bytes 73732
  265.3 1.4 collective-permute-start.3
  279.0 10.3 %all-to-all-start.8 = ((bf16[4,3,1,1024]{3,1,2,0:T(4,128)(2,1)}), bf16[4,3,1,1024]{3,1,2,0:T(4,128)(2,1)S(1)}, u32[]{:S(2)}, u32[]{:S(2)}) async-start(bf16[4,3,1,1024]{3,1,2,0:T(4,128)(2,1)} %pad_maximum_fusion.4), calls=%async_computation.8 | async-start | bytes 65536 | tf_op jit(solution)/shard_map/all_to_all | solution.py:148
  289.6 12.4 %copy-start.2 = (bf16[256,128]{1,0:T(8,128)(2,1)}, bf16[256,128]{1,0:T(8,128)(2,1)S(1)}, u32[]{:S(2)}) copy-start(bf16[256,128]{1,0:T(8,128)(2,1)S(1)} %maximum_dynamic-update-slice_fusion.4) | copy-start | bytes 196612
  290.2 11.8 %copy-start.9 = (bf16[3072,64]{0,1:T(8,128)(2,1)S(1)}, bf16[3072,64]{0,1:T(8,128)(2,1)}, u32[]{:S(2)}) copy-start(bf16[3072,64]{0,1:T(8,128)(2,1)} %param.19) | copy-start | bytes 1179652
  291.9 8.8 %all-to-all-start.9 = ((bf16[4,2,512]{2,1,0:T(2,128)(2,1)}), bf16[4,2,512]{2,1,0:T(2,128)(2,1)S(1)}, u32[]{:S(2)}, u32[]{:S(2)}) async-start(bf16[4,2,512]{2,1,0:T(2,128)(2,1)} %reshape.2987), calls=%async_computation.9 | async-start | bytes 16384 | tf_op jit(solution)/shard_map/all_to_all | solution.py:177
  295.1 30.4 %reduce-scatter.29.cloned.1.call-start = ((), (), s32[]{:S(2)}) async-start(), calls=%async_computation.19 | async-start | bytes 983040
  310.0 32.9 %copy-start.5 = (f32[1,4,16,64]{3,2,1,0:T(8,128)S(1)}, f32[1,4,16,64]{3,2,1,0:T(8,128)}, u32[]{:S(2)}) copy-start(f32[1,4,16,64]{3,2,1,0:T(8,128)} %param.13) | copy-start | bytes 49156
  326.6 8.5 %collective-permute-start.4 = (bf16[1,1,16,3072]{3,2,1,0:T(8,128)(2,1)S(1)}, bf16[1,1,16,3072]{3,2,1,0:T(8,128)(2,1)S(1)}, u32[]{:S(2)}, u32[]{:S(2)}) collective-permute-start(bf16[1,1,16,3072]{3,2,1,0:T(8,128)(2,1)S(1)} %fusion.103), channel_id=1, source_target_pairs={{0,16},{16,0},{1,17},{17,1},{2,18},{18,2},{3,19},{19,3},{4,20},{20... | collective-permute-start | bytes 294920 | tf_op jit(solution)/shard_map/ppermute | solution.py:15
Sparse Core Ops, SparseCore 0:
  59.2 25.5 reduce-scatter.20
  121.2 23.3 reduce-scatter.22
  181.0 23.3 reduce-scatter.24
  240.8 23.3 reduce-scatter.26
  302.1 23.3 reduce-scatter.28
where the time goes:
time: 353 us; the launch traced here: 352 us
  waiting for transfers between devices  139 us (39%)
  blocking collectives  119 us (34%)
  starting transfers between devices  30.2 us (9%)
  other arithmetic  28.5 us (8%)
  between operations  14.9 us (4%)
  matrix products  12 us (3%)
  local copies, waits for them, and re-layouts  8.8 us (2%)
    unnamed x10, waiting for transfers between devices  103 us
    all_gather x5, blocking collectives, spread(): return lax.all_gather(values, 'cfg', axis=0, tiled=True)  48.7 us
    all_gather x4, blocking collectives, per_device(): all_values = lax.all_gather(own_values, 'cfg', axis=0, tiled=True)  30.8 us
    all_to_all x5, waiting for transfers between devices, per_device(): lax.all_to_all(outgoing, 'seq', split_axis=0, concat_axis=3, tiled=True)  25.4 us
    all_to_all x3, blocking collectives, per_device(): lax.all_to_all(attended, 'seq', split_axis=2, concat_axis=0, tiled=True)  23.8 us
    all_to_all x5, starting transfers between devices, per_device(): lax.all_to_all(outgoing, 'seq', split_axis=0, concat_axis=3, tiled=True)  23.2 us
    all_gather x1, blocking collectives, per_device(): lax.all_gather(out_weight[0], 'seq', axis=0, tiled=True)  15.7 us
  transfers between devices with their start and end apart: 17, of which 15 were waited for; matrix products, arithmetic and copies ran while one was open for 1% of the time, Pallas kernels for 0%

commit v1 on v0

--- a/solution.py
+++ b/solution.py
@@ -109,13 +109,11 @@
         query_block = query_block // 2
     scale_factor = HD ** (-0.5)
     key_cache = stale_rows
-    received = jnp.zeros_like(hidden_states[:, :1])
-    pieces = []
-    for tick_id in range(patches + 1):
-        first_patch = jnp.clip(tick_id - section_id, 0, patches - 1)
-        source = hidden_states[:, min(tick_id, patches - 1)][:, None]
-        hidden = jnp.where(section_id == 0, source, received)
-        run_key_cache = key_cache
+    received = hidden_states
+    first_patch = 0
+    for tick_id in range(2):
+        hidden = jnp.where(section_id == 0, hidden_states, received)
+        run_key_cache = stale_rows
         patch_count = hidden.shape[1]
         row_place = (
             (first_patch + jnp.arange(patch_count))[:, None] * patch_len
@@ -183,23 +181,20 @@
             tiled=True,
         )
         result = (hidden.astype(jnp.float32) + gate_rows * update).astype(jnp.bfloat16)
-        result, key_cache = (result, run_key_cache)
-        received = handoff(result)
-        if tick_id > 0:
-            final_rows = jnp.where(section_id == 1, result, received)
-            normed = row_norm(final_rows.astype(jnp.float32))
-            normed_out = (normed * (1.0 + out_modulation[1]) + out_modulation[0]).astype(
-                jnp.bfloat16
-            )
-            own_values = jnp.einsum(
-                "sqd,do->sqo", normed_out[:, 0], proj_weight, preferred_element_type=jnp.float32
-            )
-            all_values = lax.all_gather(own_values, "cfg", axis=0, tiled=True)
-            predicted = lax.dynamic_slice_in_dim(all_values, 2 * section_id, 2, 0)
-            solver_row = solver_coef[0]
-            guided = predicted[0] + solver_row[2] * (predicted[1] - predicted[0])
-            pieces.append(solver_row[0] * latent[0, tick_id - 1] + solver_row[1] * guided)
-    new_latent = jnp.stack(pieces, axis=0)[None]
+        key_cache = jnp.where(section_id == tick_id, run_key_cache, key_cache)
+        if tick_id == 0:
+            received = handoff(result)
+    normed = row_norm(result.astype(jnp.float32))
+    normed_out = (normed * (1.0 + out_modulation[1]) + out_modulation[0]).astype(jnp.bfloat16)
+    own_values = jnp.einsum(
+        "spqd,do->spqo", normed_out, proj_weight, preferred_element_type=jnp.float32
+    )
+    all_values = lax.all_gather(own_values, ("section", "cfg"), axis=0, tiled=True)
+    last = all_values.shape[0] // 2
+    predicted = lax.dynamic_slice_in_dim(all_values, last + 2 * section_id, 2, 0)
+    solver_row = solver_coef[0]
+    guided = predicted[0] + solver_row[2] * (predicted[1] - predicted[0])
+    new_latent = (solver_row[0] * latent[0] + solver_row[1] * guided)[None]
     return (new_latent, key_cache[None, None, None])
 
 

time: 353 us -> 295 us (0.84)
  blocking collectives: 119 us -> 47.4 us
  waiting for transfers between devices: 139 us -> 159 us
  starting transfers between devices: 30.2 us -> 12.7 us
  loops' own time: 0 us -> 6.14 us
    all_gather x0 -> x2, waiting for transfers between devices: none -> 64.5 us  [spread(): return lax.all_gather(values, 'cfg', axis=0, tiled=True)]
    all_gather x9 -> x1, blocking collectives: 79.6 us -> 23.8 us  [per_device(): lax.all_gather(own_values, ('section', 'cfg'), axis=0, tiled=True)]
    unnamed x10 -> x6, waiting for transfers between devices: 103 us -> 82.5 us
    all_to_all x3 -> x1, blocking collectives: 23.8 us -> 8.01 us  [per_device(): lax.all_to_all(attended, 'seq', split_axis=2, concat_axis=0, tiled=True)]
    all_to_all x5 -> x2, waiting for transfers between devices: 25.4 us -> 10.5 us  [per_device(): lax.all_to_all(outgoing, 'seq', split_axis=0, concat_axis=3, tiled=True)]
    all_to_all x5 -> x2, starting transfers between devices: 23.2 us -> 9.2 us  [per_device(): lax.all_to_all(outgoing, 'seq', split_axis=0, concat_axis=3, tiled=True)]
    select_n x1 -> x8, other arithmetic: 1.34 us -> 10.3 us  [per_device(): jnp.where(row_ids < TEXT, row_ids < text_limit, row_ids - TEXT < video_li...]
    another operation x0 -> x2, loops' own time: none -> 6.14 us  [per_device(): lax.map(attend, (incoming[0].reshape(block_count, query_block, HD), jnp.a...]
  transfers between devices with their start and end apart: 17 -> 8, of which waited for: 15 -> 7; matrix products, arithmetic and copies ran while one was open for 1% -> 1% of each run, Pallas kernels for 0% -> 0%
where the time goes in v1:
time: 295 us; the launch traced here: 294 us
  waiting for transfers between devices  159 us (54%)
  blocking collectives  47.4 us (16%)
  other arithmetic  29 us (10%)
  between operations  14.3 us (5%)
  matrix products  13.4 us (5%)
  starting transfers between devices  12.7 us (4%)
  local copies, waits for them, and re-layouts  11.7 us (4%)
  loops' own time  6.14 us (2%)
    unnamed x6, waiting for transfers between devices  82.5 us
    all_gather x2, waiting for transfers between devices, spread(): return lax.all_gather(values, 'cfg', axis=0, tiled=True)  64.5 us
    all_gather x1, blocking collectives, per_device(): lax.all_gather(own_values, ('section', 'cfg'), axis=0, tiled=True)  23.8 us
    all_gather x1, blocking collectives, per_device(): lax.all_gather(out_weight[0], 'seq', axis=0, tiled=True)  15.5 us
    all_to_all x2, waiting for transfers between devices, per_device(): lax.all_to_all(outgoing, 'seq', split_axis=0, concat_axis=3, tiled=True)  10.5 us
    select_n x8, other arithmetic, per_device(): jnp.where(row_ids < TEXT, row_ids < text_limit, row_ids - TEXT < video_li...  10.3 us
    all_to_all x2, starting transfers between devices, per_device(): lax.all_to_all(outgoing, 'seq', split_axis=0, concat_axis=3, tiled=True)  9.2 us
    all_to_all x1, blocking collectives, per_device(): lax.all_to_all(attended, 'seq', split_axis=2, concat_axis=0, tiled=True)  8.01 us
  transfers between devices with their start and end apart: 8, of which 7 were waited for; matrix products, arithmetic and copies ran while one was open for 1% of the time, Pallas kernels for 0%

profile of v1, /device:TPU:0, one launch (start us, length us, event | category | flops | bytes accessed | tf_op | source)
XLA Modules:
  0.0 293.7 jit_solution(7115871315893856037)
XLA Ops:
  9.3 1.2 fusion.56
  10.5 2.0 fusion.62
  13.0 33.4 %all-gather.5.cloned.1.call-done = bf16[4,4,16,3072]{3,2,1,0:T(8,128)(2,1)} async-done(((bf16[1,4,16,3072]{3,2,1,0:T(8,128)(2,1)}), bf16[4,4,16,3072]{3,2,1,0:T(8,128)(2,1)}) %all-gather.5.cloned.1.call-update) | async-done | bytes 1572880 | tf_op jit(solution)/shard_map/all_gather | solution.py:65
  46.4 2.4 fusion.43
  51.0 4.6 %all-to-all-start = ((bf16[4,3,4,1024]{3,2,1,0:T(4,128)(2,1)}), bf16[4,3,4,1024]{3,2,1,0:T(4,128)(2,1)S(1)}, u32[]{:S(2)}, u32[]{:S(2)}) async-start(bf16[4,3,4,1024]{3,2,1,0:T(4,128)(2,1)} %pad_maximum_fusion), calls=%async_computation | async-start | bytes 196608 | tf_op jit(solution)/shard_map/all_to_all | solution.py:146
  56.8 4.6 %all-to-all-done = bf16[4,3,4,1024]{3,2,1,0:T(4,128)(2,1)S(1)} async-done(((bf16[4,3,4,1024]{3,2,1,0:T(4,128)(2,1)}), bf16[4,3,4,1024]{3,2,1,0:T(4,128)(2,1)S(1)}, u32[]{:S(2)}, u32[]{:S(2)}) %all-to-all-start) | async-done | bytes 98336 | tf_op jit(solution)/shard_map/all_to_all | solution.py:146
  62.1 14.0 %while.26 = (s32[]{:T(128)}, bf16[4,64,64]{2,1,0:T(8,128)(2,1)S(1)}, bf16[4,64,64]{2,1,0:T(8,128)(2,1)S(1)}, s32[4]{0:T(128)S(1)}, bf16[256,128]{1,0:T(8,128)(2,...) while((s32[]{:T(128)}, ...), condition=%wide.region_9.10_spmd.clone, body=%wide.region_6.9_spmd.clone.sunk | while | flops 4353426 | bytes 560455 | solution.py:171
  63.6 1.3 compare_select_fusion.4
  67.1 1.3 compare_select_fusion.4
  70.6 1.3 compare_select_fusion.4
  74.1 1.3 compare_select_fusion.4
  76.8 3.3 %all-to-all-start.1 = ((bf16[1,4,4,1024]{3,1,0,2:T(4,128)(2,1)}), bf16[1,4,4,1024]{3,1,0,2:T(4,128)(2,1)S(1)}, u32[]{:S(2)}, u32[]{:S(2)}) async-start(bf16[1,4,4,1024]{3,1,0,2:T(4,128)(2,1)} %copy.60), calls=%async_computation.1 | async-start | bytes 65536 | tf_op jit(solution)/shard_map/all_to_all | solution.py:175
  80.2 15.5 %all-gather = bf16[1,3072,64]{1,2,0:T(8,128)(2,1)S(1)} all-gather(bf16[1,768,64]{1,2,0:T(8,128)(2,1)S(1)} %copy-done.3), channel_id=2, replica_groups=mesh['section'=2,'seq'=4,'cfg'=4] {'seq'}, dimensions={1}, use_global_device_ids=true | all-gather | bytes 491520 | tf_op jit(solution)/shard_map/all_gather | solution.py:96
  95.8 2.2 fusion.72
  98.1 43.4 %reduce-scatter.7.cloned.1.call-done = f32[1,4,16,3072]{3,2,1,0:T(8,128)} async-done(((f32[4,4,16,3072]{3,2,1,0:T(8,128)}), f32[1,4,16,3072]{3,2,1,0:T(8,128)}) %reduce-scatter.7.cloned.1.call-update) | async-done | bytes 786448
  141.5 1.3 fusion.64
  142.9 1.7 collective-permute-done
  146.1 31.1 %all-gather.7.cloned.1.call-done = bf16[4,4,16,3072]{3,2,1,0:T(8,128)(2,1)} async-done(((bf16[1,4,16,3072]{3,2,1,0:T(8,128)(2,1)}), bf16[4,4,16,3072]{3,2,1,0:T(8,128)(2,1)}) %all-gather.7.cloned.1.call-update) | async-done | bytes 1572880 | tf_op jit(solution)/shard_map/all_gather | solution.py:65
  177.3 2.4 fusion.40
  181.7 4.6 %all-to-all-start.2 = ((bf16[4,3,4,1024]{3,2,1,0:T(4,128)(2,1)}), bf16[4,3,4,1024]{3,2,1,0:T(4,128)(2,1)S(1)}, u32[]{:S(2)}, u32[]{:S(2)}) async-start(bf16[4,3,4,1024]{3,2,1,0:T(4,128)(2,1)} %pad_maximum_fusion.1), calls=%async_computation.2 | async-start | bytes 196608 | tf_op jit(solution)/shard_map/all_to_all | solution.py:146
  186.3 5.8 %all-to-all-done.2 = bf16[4,3,4,1024]{3,2,1,0:T(4,128)(2,1)S(1)} async-done(((bf16[4,3,4,1024]{3,2,1,0:T(4,128)(2,1)}), bf16[4,3,4,1024]{3,2,1,0:T(4,128)(2,1)S(1)}, u32[]{:S(2)}, u32[]{:S(2)}) %all-to-all-start.2) | async-done | bytes 98336 | tf_op jit(solution)/shard_map/all_to_all | solution.py:146
  192.8 14.0 %while.27 = (s32[]{:T(128)}, bf16[4,64,64]{2,1,0:T(8,128)(2,1)S(1)}, bf16[4,64,64]{2,1,0:T(8,128)(2,1)S(1)}, s32[4]{0:T(128)S(1)}, bf16[256,128]{1,0:T(8,128)(2,...) while((s32[]{:T(128)}, ...), condition=%wide.region_20.21_spmd.clone, body=%wide.region_17.20_spmd.clone.sunk | while | flops 4353426 | bytes 560455 | solution.py:171
  194.3 1.3 compare_select_fusion.5
  197.8 1.3 compare_select_fusion.5
  201.3 1.3 compare_select_fusion.5
  204.8 1.3 compare_select_fusion.5
  206.9 8.0 %all_to_all.60 = bf16[1,4,4,1024]{3,1,0,2:T(4,128)(2,1)S(1)} all-to-all(bf16[1,4,4,1024]{3,1,0,2:T(4,128)(2,1)S(1)} %copy.67), channel_id=1, replica_groups=mesh['section'=2,'seq'=4,'cfg'=4] {'seq'}, dimensions={2} | all-to-all | bytes 65536 | tf_op jit(solution)/shard_map/all_to_all | solution.py:175
  215.0 2.2 fusion.70
  219.8 39.1 %reduce-scatter.9.cloned.1.call-done = f32[1,4,16,3072]{3,2,1,0:T(8,128)} async-done(((f32[4,4,16,3072]{3,2,1,0:T(8,128)}), f32[1,4,16,3072]{3,2,1,0:T(8,128)}) %reduce-scatter.9.cloned.1.call-update) | async-done | bytes 786448
  258.8 1.4 convert_reduce_fusion.2
  260.9 23.8 %all-gather.1 = f32[32,16,64]{2,1,0:T(8,128)S(1)} all-gather(f32[4,16,64]{2,1,0:T(8,128)S(1)} %fusion.67), channel_id=3, replica_groups=mesh['section'=2,'seq'=4,'cfg'=4] {'section','cfg'}, dimensions={0}, use_global_device_ids=true | all-gather | bytes 147456 | tf_op jit(solution)/shard_map/all_gather | solution.py:192
  284.7 2.5 fusion.103
  (166 shorter events, 26.4 us)
Async XLA Ops:
  7.2 39.3 %copy-start = (bf16[1,3072,3,64]{1,3,2,0:T(8,128)(2,1)S(1)}, bf16[1,3072,3,64]{1,3,2,0:T(8,128)(2,1)}, u32[]{:S(2)}) copy-start(bf16[1,3072,3,64]{1,3,2,0:T(8,128)(2,1)} %param.19) | copy-start | bytes 3538948
  7.2 5.4 %copy-start.6 = (s32[3,2,4,16]{3,2,1,0:T(4,128)S(1)}, s32[3,2,4,16]{3,2,1,0:T(4,128)}, u32[]{:S(2)}) copy-start(s32[3,2,4,16]{3,2,1,0:T(4,128)} %param.27) | copy-start | bytes 4612
  7.2 39.2 %all-gather.5.cloned.1.call-start = ((), (), s32[]{:S(2)}) async-start(), calls=%async_computation.6 | async-start | bytes 1966080 | tf_op jit(solution)/shard_map/all_gather | solution.py:65
  49.1 6.6 %copy-start.9 = (s32[2]{0:T(128)S(1)}, s32[2]{0:T(128)}, u32[]{:S(2)}) copy-start(s32[2]{0:T(128)} %param.25) | copy-start | bytes 28
  49.1 7.2 %copy-start.10 = (s32[4]{0:T(128)S(1)}, s32[4]{0:T(128)}, u32[]{:S(2)}) copy-start(s32[4]{0:T(128)} %param.26) | copy-start | bytes 52
  49.6 12.4 %copy-start.2 = (bf16[1,1,1,256,128]{4,3,2,1,0:T(8,128)(2,1)S(1)}, bf16[1,1,1,256,128]{4,3,2,1,0:T(8,128)(2,1)}, u32[]{:S(2)}) copy-start(bf16[1,1,1,256,128]{4,3,2,1,0:T(8,128)(2,1)} %param.18) | copy-start | bytes 196612
  51.0 10.4 %all-to-all-start = ((bf16[4,3,4,1024]{3,2,1,0:T(4,128)(2,1)}), bf16[4,3,4,1024]{3,2,1,0:T(4,128)(2,1)S(1)}, u32[]{:S(2)}, u32[]{:S(2)}) async-start(bf16[4,3,4,1024]{3,2,1,0:T(4,128)(2,1)} %pad_maximum_fusion), calls=%async_computation | async-start | bytes 196608 | tf_op jit(solution)/shard_map/all_to_all | solution.py:146
  62.1 18.1 %copy-start.3 = (bf16[1,768,64]{1,2,0:T(8,128)(2,1)S(1)}, bf16[1,768,64]{1,2,0:T(8,128)(2,1)}, u32[]{:S(2)}) copy-start(bf16[1,768,64]{1,2,0:T(8,128)(2,1)} %param.20) | copy-start | bytes 294916
  76.8 18.9 %all-to-all-start.1 = ((bf16[1,4,4,1024]{3,1,0,2:T(4,128)(2,1)}), bf16[1,4,4,1024]{3,1,0,2:T(4,128)(2,1)S(1)}, u32[]{:S(2)}, u32[]{:S(2)}) async-start(bf16[1,4,4,1024]{3,1,0,2:T(4,128)(2,1)} %copy.60), calls=%async_computation.1 | async-start | bytes 65536 | tf_op jit(solution)/shard_map/all_to_all | solution.py:175
  80.1 61.4 %reduce-scatter.7.cloned.1.call-start = ((), (), s32[]{:S(2)}) async-start(), calls=%async_computation.8 | async-start | bytes 3932160
  98.0 43.4 %copy-start.1 = (bf16[1,4,16,3072]{3,2,1,0:T(8,128)(2,1)S(1)}, bf16[1,4,16,3072]{3,2,1,0:T(8,128)(2,1)}, u32[]{:S(2)}) copy-start(bf16[1,4,16,3072]{3,2,1,0:T(8,128)(2,1)} %param.16) | copy-start | bytes 1179652
  98.1 79.2 %all-gather.7.cloned.1.call-start = ((), (), s32[]{:S(2)}) async-start(), calls=%async_computation.7 | async-start | bytes 1966080 | tf_op jit(solution)/shard_map/all_gather | solution.py:65
  142.8 1.8 collective-permute-start
  181.7 10.4 %all-to-all-start.2 = ((bf16[4,3,4,1024]{3,2,1,0:T(4,128)(2,1)}), bf16[4,3,4,1024]{3,2,1,0:T(4,128)(2,1)S(1)}, u32[]{:S(2)}, u32[]{:S(2)}) async-start(bf16[4,3,4,1024]{3,2,1,0:T(4,128)(2,1)} %pad_maximum_fusion.1), calls=%async_computation.2 | async-start | bytes 196608 | tf_op jit(solution)/shard_map/all_to_all | solution.py:146
  186.3 72.5 %reduce-scatter.9.cloned.1.call-start = ((), (), s32[]{:S(2)}) async-start(), calls=%async_computation.9 | async-start | bytes 3932160
  217.3 0.7 copy-start.7
  217.3 1.3 copy-start.5
  217.3 43.3 %copy-start.8 = (bf16[3072,64]{0,1:T(8,128)(2,1)S(1)}, bf16[3072,64]{0,1:T(8,128)(2,1)}, u32[]{:S(2)}) copy-start(bf16[3072,64]{0,1:T(8,128)(2,1)} %param.23) | copy-start | bytes 1179652
  219.8 64.9 %copy-start.4 = (f32[1,4,16,64]{3,2,1,0:T(8,128)S(1)}, f32[1,4,16,64]{3,2,1,0:T(8,128)}, u32[]{:S(2)}) copy-start(f32[1,4,16,64]{3,2,1,0:T(8,128)} %param.17) | copy-start | bytes 49156
Sparse Core Ops, SparseCore 0:
  12.7 33.6 all-gather.4
  98.2 43.2 reduce-scatter.6
  146.3 30.9 all-gather.6
  217.4 41.3 reduce-scatter.8

commit v2 on v1

--- a/solution.py
+++ b/solution.py
@@ -3,6 +3,8 @@
 import jax
 import jax.numpy as jnp
 from jax import lax
+from jax.experimental import pallas as pl
+from jax.experimental.pallas import tpu as pltpu
 from jax.sharding import PartitionSpec as P
 
 HD = 64
@@ -69,7 +71,7 @@
     return from_behind(values, "section", 1)
 
 
-def per_device(
+def general(
     hidden_states,
     latent,
     stale_cache,
@@ -198,6 +200,372 @@
     return (new_latent, key_cache[None, None, None])
 
 
+def fused_kernel(
+    hid, lat, stale, wqkv, wout, mod, omod, proj, coef, cos_t, sin_t, bias,
+    lat_out, cache_out,
+    x_buf, mix, qkv_out, qkv_in, att_out, att_in, wo, mod0, fin, pred, pred_in,
+    g_s, g_r, q_s, q_r, a_s, a_r, w_s, w_r, f_s, f_r, m_s, m_r, p_s, p_r, go,
+):
+    sec = lax.axis_index("section")
+    z = lax.axis_index("seq")
+    c = lax.axis_index("cfg")
+    width = hid.shape[1]
+    shard = wout.shape[1]
+    count = 4
+
+    def place(section, seq, cfg):
+        return {"section": section, "seq": seq, "cfg": cfg}
+
+    def remote(src, dst, send, recv, target):
+        return pltpu.make_async_remote_copy(
+            src_ref=src, dst_ref=dst, send_sem=send, recv_sem=recv,
+            device_id=target, device_id_type=pl.DeviceIdType.MESH,
+        )
+
+    def landed(dst, sem):
+        pltpu.make_async_copy(dst, dst, sem).wait()
+
+    barrier = pltpu.get_barrier_semaphore()
+    everyone = 2 * count * count
+    me = (sec * count + z) * count + c
+
+    def greet(i, carry):
+        other = lax.rem(me + i, everyone)
+        pl.semaphore_signal(
+            barrier, inc=1,
+            device_id=place(other // 16, lax.rem(other // 4, 4), lax.rem(other, 4)),
+            device_id_type=pl.DeviceIdType.MESH,
+        )
+        return carry
+
+    lax.fori_loop(1, everyone, greet, 0)
+    pl.semaphore_wait(barrier, everyone - 1)
+
+    own_cols = pl.ds(pl.multiple_of(z * shard, 128), shard)
+
+    def shard_copy(layer, k):
+        return remote(
+            wout, wo.at[layer, c, :, own_cols], w_s.at[k], w_r.at[layer, z],
+            place(1, lax.rem(z + k, 4), c),
+        )
+
+    def forward(layer, k):
+        return remote(
+            wo.at[layer, c], wo.at[layer, c], f_s.at[layer, k - 1], f_r.at[layer, k - 1],
+            place(1, z, lax.rem(c + k, 4)),
+        )
+
+    def shards_landed(layer):
+        for zz in range(count):
+            dst = wo.at[layer, c, :, zz * shard : (zz + 1) * shard]
+            if layer == 0:
+                landed(dst, w_r.at[layer, zz])
+            else:
+                @pl.when(z != zz)
+                def _():
+                    landed(dst, w_r.at[layer, zz])
+
+    def forwards_landed(layer):
+        for k in range(1, count):
+            landed(wo.at[layer, lax.rem(c + 4 - k, 4)], f_r.at[layer, k - 1])
+
+    def text_mask(start, rows):
+        i = lax.broadcasted_iota(jnp.int32, (rows, 1), 0) + start
+        return (i // 16) * 64 + z * 16 + i % 16 < TEXT
+
+    def norm16(values):
+        values = values.astype(jnp.float32)
+        centered = values - jnp.mean(values, axis=-1, keepdims=True)
+        return centered * lax.rsqrt(jnp.mean(centered * centered, axis=-1, keepdims=True) + 1e-05)
+
+    def out_projection(layer, prev, gates):
+        for h in range(count):
+            landed(att_in.at[layer, h], a_r.at[layer, h])
+        rows = [att_in[layer, h].reshape(64, 128)[:, HD:] for h in range(count)]
+        joined = jnp.concatenate(rows, axis=1)
+        text = text_mask(0, 64)
+        for part in range(4):
+            cols = slice(part * (width // 4), (part + 1) * (width // 4))
+            weight = wo[layer, :, :, cols].reshape(4 * HD, width // 4)
+            update = jnp.dot(joined, weight, preferred_element_type=jnp.float32)
+            gate = jnp.where(text, gates[5:6, cols], gates[2:3, cols])
+            x_buf[:, cols] = (prev[:, cols].astype(jnp.float32) + gate * update).astype(jnp.bfloat16)
+
+    mod_copy = remote(mod, mod0, m_s, m_r, place(1, z, c))
+
+    @pl.when(sec == 0)
+    def _():
+        mod_copy.start()
+        for k in range(count):
+            shard_copy(0, k).start()
+        x_buf[...] = hid[...]
+
+    @pl.when(sec == 1)
+    def _():
+        for k in range(1, count):
+            shard_copy(1, k).start()
+        wo[1, c, :, own_cols] = wout[...]
+        shards_landed(0)
+        pl.semaphore_wait(go, 1)
+        for k in range(1, count):
+            forward(0, k).start()
+        shards_landed(1)
+        mod_copy.wait_recv()
+        forwards_landed(0)
+        out_projection(0, hid, mod0)
+
+    def mix_rows(p, carry):
+        rows = pl.ds(pl.multiple_of(p * 16, 16), 16)
+        text = text_mask(p * 16, 16)
+        normed = norm16(x_buf[rows, :])
+        scale = jnp.where(text, mod[4:5, :], mod[1:2, :])
+        shift = jnp.where(text, mod[3:4, :], mod[0:1, :])
+        mix[c, rows, :] = (normed * (1.0 + scale) + shift).astype(jnp.bfloat16)
+        return carry
+
+    lax.fori_loop(0, 4, mix_rows, 0)
+
+    def gather(k):
+        return remote(
+            mix.at[c], mix.at[c], g_s.at[k - 1], g_r.at[k - 1], place(sec, z, lax.rem(c + k, 4))
+        )
+
+    for k in range(1, count):
+        gather(k).start()
+
+    lane = lax.broadcasted_iota(jnp.int32, (1, 128), 1)
+    head = lane < HD
+    low = (lane // 32) % 2 == 0
+
+    def prepare(values, cos_table, sin_table):
+        mean = jnp.sum(jnp.where(head, values, 0.0), axis=-1, keepdims=True) * (1.0 / HD)
+        centered = values - mean
+        square = jnp.where(head, centered * centered, 0.0)
+        scale = lax.rsqrt(jnp.sum(square, axis=-1, keepdims=True) * (1.0 / HD) + 1e-06)
+        normed = jnp.where(head, centered * scale, values)
+        swapped = jnp.where(low, pltpu.roll(normed, 96, 1), pltpu.roll(normed, 32, 1))
+        return (normed * cos_table + swapped * sin_table).astype(jnp.bfloat16).reshape(4, 16, 128)
+
+    def qkv_copy(s):
+        return remote(
+            qkv_out.at[s], qkv_in.at[:, z], q_s.at[s], q_r.at[z], place(sec, s, c)
+        )
+
+    for k in range(count):
+        s = lax.rem(c + 4 - k, 4)
+        if k > 0:
+            landed(mix.at[s], g_r.at[k - 1])
+        projected = jnp.dot(mix[s], wqkv[...], preferred_element_type=jnp.float32)
+        cos_table = cos_t[s // 2]
+        sin_table = sin_t[s // 2]
+        kv = prepare(projected[:, :128], cos_table, sin_table)
+        qq = prepare(projected[:, 128:], cos_table, sin_table)
+
+        qkv_out[s, :, :, :128] = kv
+        qkv_out[s, :, :, 128:] = qq
+
+        @pl.when(s != z)
+        def _():
+            qkv_copy(s).start()
+
+    @pl.when(sec == 0)
+    def _():
+        pl.semaphore_signal(
+            go, inc=1, device_id=place(1, z, c), device_id_type=pl.DeviceIdType.MESH
+        )
+
+    @pl.when(sec == 1)
+    def _():
+        for k in range(1, count):
+            forward(1, k).start()
+
+    qkv_in[:, z] = qkv_out[z]
+    for k in range(1, count):
+        zz = lax.rem(z + k, 4)
+        landed(qkv_in.at[:, zz], q_r.at[zz])
+    fresh = qkv_in[:, :, :, :128].reshape(256, 128)
+    query = qkv_in[:, :, :, 128:].reshape(256, 128)[:, :HD]
+    cache_out[...] = fresh
+    old = stale[...]
+    contract = (((1,), (1,)), ((), ()))
+    fresh_scores = lax.dot_general(query, fresh[:, :HD], contract, preferred_element_type=jnp.float32)
+    old_scores = lax.dot_general(query, old[:, :HD], contract, preferred_element_type=jnp.float32)
+    query_patch = lax.broadcasted_iota(jnp.int32, (256, 256), 0) // 64
+    key_patch = lax.broadcasted_iota(jnp.int32, (256, 256), 1) // 64
+    is_fresh = key_patch <= query_patch
+    scores = jnp.where(is_fresh, fresh_scores, old_scores) * (HD ** -0.5) + bias[0:1, :]
+    weights = jnp.exp(scores - jnp.max(scores, axis=1, keepdims=True))
+    total = jnp.sum(weights, axis=1, keepdims=True)
+    combined = jnp.dot(
+        jnp.where(is_fresh, weights, 0.0).astype(jnp.bfloat16), fresh,
+        preferred_element_type=jnp.float32,
+    ) + jnp.dot(
+        jnp.where(is_fresh, 0.0, weights).astype(jnp.bfloat16), old,
+        preferred_element_type=jnp.float32,
+    )
+    att_out[...] = (combined / total).astype(jnp.bfloat16).reshape(4, 4, 16, 128)
+
+    def att_copy(zz):
+        return remote(
+            att_out.at[:, zz], att_in.at[sec, c], a_s.at[zz], a_r.at[sec, c], place(1, zz, z)
+        )
+
+    def own_copy(zz):
+        return pltpu.make_async_copy(att_out.at[:, zz], att_in.at[1, c], a_r.at[1, c])
+
+    for zz in range(count):
+        stays = jnp.logical_and(sec == 1, jnp.logical_and(z == zz, c == z))
+
+        @pl.when(stays)
+        def _():
+            own_copy(zz).start()
+
+        @pl.when(jnp.logical_not(stays))
+        def _():
+            att_copy(zz).start()
+
+    def pred_copy(k):
+        return remote(
+            pred, pred_in.at[c % 2], p_s.at[k], p_r.at[c % 2],
+            place(c // 2, z, lax.rem(c + k, 4)),
+        )
+
+    @pl.when(sec == 1)
+    def _():
+        forwards_landed(1)
+        out_projection(1, x_buf, mod)
+
+        def last_rows(p, carry):
+            rows = pl.ds(pl.multiple_of(p * 16, 16), 16)
+            normed = norm16(x_buf[rows, :])
+            fin[rows, :] = (normed * (1.0 + omod[1:2, :]) + omod[0:1, :]).astype(jnp.bfloat16)
+            return carry
+
+        lax.fori_loop(0, 4, last_rows, 0)
+        pred[...] = jnp.dot(fin[...], proj[...], preferred_element_type=jnp.float32)
+
+        @pl.when(c // 2 == 0)
+        def _():
+            pred_copy(0).start()
+
+        @pl.when(c // 2 == 1)
+        def _():
+            pltpu.make_async_copy(pred, pred_in.at[c % 2], p_r.at[c % 2]).start()
+
+        for k in range(1, count):
+            pred_copy(k).start()
+
+    for half in range(2):
+        landed(pred_in.at[half], p_r.at[half])
+    first = pred_in[0]
+    guided = first + coef[0, 2] * (pred_in[1] - first)
+    lat_out[...] = coef[0, 0] * lat[...] + coef[0, 1] * guided
+
+    @pl.when(sec == 0)
+    def _():
+        mod_copy.wait_send()
+        for k in range(count):
+            shard_copy(0, k).wait_send()
+
+    @pl.when(sec == 1)
+    def _():
+        for k in range(1, count):
+            shard_copy(1, k).wait_send()
+            forward(0, k).wait_send()
+            forward(1, k).wait_send()
+            pred_copy(k).wait_send()
+
+        @pl.when(c // 2 == 0)
+        def _():
+            pred_copy(0).wait_send()
+
+    for k in range(1, count):
+        gather(k).wait_send()
+        qkv_copy(lax.rem(z + k, 4)).wait_send()
+    for zz in range(count):
+        stays = jnp.logical_and(sec == 1, jnp.logical_and(z == zz, c == z))
+
+        @pl.when(jnp.logical_not(stays))
+        def _():
+            att_copy(zz).wait_send()
+
+
+def fused(
+    hidden_states, latent, stale_cache, qkv_weight, out_weight, modulation, out_modulation,
+    proj_weight, solver_coef, video_len, text_len, positions,
+):
+    z = lax.axis_index("seq")
+    width = hidden_states.shape[3]
+    qkv = qkv_weight[0]
+    wqkv = jnp.concatenate(
+        [qkv[:, 1], qkv[:, 2], qkv[:, 0], jnp.zeros_like(qkv[:, 0])], axis=1
+    )
+    wout = out_weight[0].T
+    rows = jnp.arange(64)
+    row_place = (rows // 16) * 64 + z * 16 + rows % 16
+    places = positions.reshape(3, 2, 64).astype(jnp.float32)
+    angles = rope_angles(places, HD)
+    angles = jnp.where((row_place < TEXT)[None, :, None], 0.0, angles)
+    cos, sin = jnp.cos(angles), jnp.sin(angles)
+    rest = jnp.zeros((2, 64, HD), jnp.float32)
+    cos_t = jnp.concatenate([cos, cos, rest + 1.0], axis=-1)
+    sin_t = jnp.concatenate([-sin, sin, rest], axis=-1)
+    row_ids = jnp.arange(256)
+    text_limit = lax.dynamic_index_in_dim(text_len, z, keepdims=False)
+    video_limit = lax.dynamic_index_in_dim(video_len, z // 2, keepdims=False)
+    live = jnp.where(row_ids < TEXT, row_ids < text_limit, row_ids - TEXT < video_limit)
+    bias = jnp.where(live, 0.0, -jnp.inf).astype(jnp.float32)[None]
+    vmem = pl.BlockSpec(memory_space=pltpu.VMEM)
+    smem = pl.BlockSpec(memory_space=pltpu.SMEM)
+    dma = pltpu.SemaphoreType.DMA
+    bf16, f32 = jnp.bfloat16, jnp.float32
+    new_latent, new_cache = pl.pallas_call(
+        fused_kernel,
+        out_shape=(
+            jax.ShapeDtypeStruct((64, 64), f32),
+            jax.ShapeDtypeStruct((256, 128), bf16),
+        ),
+        in_specs=[vmem] * 8 + [smem] + [vmem] * 3,
+        out_specs=(vmem, vmem),
+        scratch_shapes=[
+            pltpu.VMEM((64, width), bf16),
+            pltpu.VMEM((4, 64, width), bf16),
+            pltpu.VMEM((4, 4, 16, 256), bf16),
+            pltpu.VMEM((4, 4, 16, 256), bf16),
+            pltpu.VMEM((4, 4, 16, 128), bf16),
+            pltpu.VMEM((2, 4, 4, 16, 128), bf16),
+            pltpu.VMEM((2, 4, HD, width), bf16),
+            pltpu.VMEM((6, width), f32),
+            pltpu.VMEM((64, width), bf16),
+            pltpu.VMEM((64, 64), f32),
+            pltpu.VMEM((2, 64, 64), f32),
+            dma((3,)), dma((3,)), dma((4,)), dma((4,)), dma((4,)), dma((2, 4)),
+            dma((4,)), dma((2, 4)), dma((2, 3)), dma((2, 3)), dma, dma, dma((4,)), dma((2,)),
+            pltpu.SemaphoreType.REGULAR,
+        ],
+        compiler_params=pltpu.CompilerParams(
+            collective_id=0, has_side_effects=True, vmem_limit_bytes=40 * 1024 * 1024
+        ),
+    )(
+        hidden_states.reshape(64, width), latent.reshape(64, 64), stale_cache[0, 0, 0], wqkv, wout,
+        modulation[0], out_modulation, proj_weight, solver_coef, cos_t, sin_t, bias,
+    )
+    return new_latent.reshape(latent.shape), new_cache.reshape(stale_cache.shape)
+
+
+def per_device(*args):
+    hidden_states, latent, stale_cache, qkv_weight = args[:4]
+    sizes = tuple(lax.axis_size(axis) for axis in ("section", "seq", "cfg"))
+    small = (
+        sizes == (2, 4, 4)
+        and hidden_states.shape[:3] == (1, 4, 16)
+        and latent.shape == (1, 4, 16, 64)
+        and stale_cache.shape == (1, 1, 1, 256, 128)
+        and qkv_weight.shape[3] == HD
+    )
+    return fused(*args) if small else general(*args)
+
+
 def solution(mesh):
     return jax.shard_map(
         per_device,

time: 295 us -> 72.7 us (0.25)
  waiting for transfers between devices: 159 us -> 0 us
  Pallas kernels: 0 us -> 61.5 us
  blocking collectives: 47.4 us -> 0 us
  other arithmetic: 29 us -> 2.82 us
  between operations: 14.3 us -> 0.88 us
  matrix products: 13.4 us -> 0 us
  starting transfers between devices: 12.7 us -> 0 us
  loops' own time: 6.14 us -> 0 us
  local copies, waits for them, and re-layouts: 11.7 us -> 7.27 us
    unnamed x6 -> x0, waiting for transfers between devices: 82.5 us -> none
    all_gather x2 -> x0, waiting for transfers between devices: 64.5 us -> none  [spread(): return lax.all_gather(values, 'cfg', axis=0, tiled=True)]
    pallas_call x0 -> x1, Pallas kernels: none -> 61.5 us  [fused(): pl.pallas_call(fused_kernel, out_shape=(jax.ShapeDtypeStruct((64, 64), f3...]
    all_gather x2 -> x0, blocking collectives: 39.3 us -> none  [the longest x1 23.8 us: per_device(): lax.all_gather(own_values, ('section', 'cfg'), axis=0, tiled=True)]
    dot_general x21 -> x0, matrix products: 13.4 us -> none  [the longest x2 4.76 us: per_device(): jnp.einsum('spqd,djge->sgjpqe', mixed_rows, qkv_full, preferred_element_t...]
    all_to_all x3 -> x0, starting transfers between devices: 12.5 us -> none  [the longest x2 9.2 us: per_device(): lax.all_to_all(outgoing, 'seq', split_axis=0, concat_axis=3, tiled=True)]
    select_n x17 -> x1, other arithmetic: 11.8 us -> 1.3 us  [fused(): bias = jnp.where(live, 0.0, -jnp.inf).astype(jnp.float32)[None]]
    all_to_all x3 -> x0, waiting for transfers between devices: 10.5 us -> none  [the longest x2 10.5 us: per_device(): lax.all_to_all(outgoing, 'seq', split_axis=0, concat_axis=3, tiled=True)]
  transfers between devices with their start and end apart: 8 -> 0, of which waited for: 7 -> 0; matrix products, arithmetic and copies ran while one was open for 1% -> 0% of each run, Pallas kernels for 0% -> 0%
where the time goes in v2:
time: 72.7 us; the launch traced here: 72.5 us
  Pallas kernels  61.5 us (85%)
  local copies, waits for them, and re-layouts  7.27 us (10%)
  other arithmetic  2.82 us (4%)
  between operations  0.88 us (1%)
    pallas_call x1, Pallas kernels, fused(): pl.pallas_call(fused_kernel, out_shape=(jax.ShapeDtypeStruct((64, 64), f3...  61.5 us
    unnamed x25, local copies, waits for them, and re-layouts  5.46 us

profile of v2, /device:TPU:0, one launch (start us, length us, event | category | flops | bytes accessed | tf_op | source)
XLA Modules:
  0.0 72.5 jit_solution(13319183180270411452)
XLA Ops:
  0.6 2.8 %copy.14 = bf16[1,3072,3,64]{3,1,2,0:T(8,128)(2,1)S(1)} copy(bf16[1,3072,3,64]{1,3,2,0:T(8,128)(2,1)} %param.15) | data formatting | bytes 2359296 | tf_op args[3]
  3.4 0.2 slice_bitcast_fusion.2
  3.6 0.0 copy-start.6
  3.6 0.1 pad.9.clone
  3.7 0.0 copy-start.1
  3.7 0.0 copy-start.2
  3.7 0.0 copy-start.3
  3.7 0.0 copy-start.4
  3.7 0.0 copy-start.5
  3.7 1.0 %maximum_maximum_fusion.wqkv = bf16[3072,256]{1,0:T(8,128)(2,1)S(1)} fusion(bf16[3072,64]{1,0:T(8,128)(2,1)S(1)} %get-tuple-element.7, bf16[3072,64]{1,0:T(8,128)(2,1)S(1)} %get-tuple-element.8, bf16[3072,64]{1,0:T(8,128)(2,1)S(1)} %get-tuple-element.6, bf16[256]{0:T(256)(128)(2,1)S(1)} %pad.9.clone), kind=kLoop, calls=%fused_computation | loop fusion | flops 6291456 | bytes 2753024 | tf_op jit(solution)/shard_map/concatenate | solution.py:500
  4.8 0.0 copy-done.6
  4.8 1.4 %copy.15.proj = bf16[3072,64]{1,0:T(8,128)(2,1)S(1)} copy(bf16[3072,64]{0,1:T(8,128)(2,1)} %param.19) | data formatting | bytes 786432 | tf_op args[7]
  6.2 0.1 mul.87
  6.3 0.1 mul.83
  6.4 0.1 mul.79
  6.5 0.4 fusion.10
  6.9 0.1 pad.5.clone
  7.0 0.1 pad.2.clone
  7.0 0.1 maximum_maximum_fusion.1
  7.2 0.6 dynamic_slice.9
  7.8 0.0 copy-done.9
  7.8 0.6 dynamic_slice.8
  8.3 1.3 %select_select_fusion.bias = f32[1,256]{1,0:T(1,128)S(1)} fusion(s32[]{:T(128)} %bitcast.10, s32[]{:T(128)} %bitcast.9), kind=kLoop, calls=%fused_computation.10 | loop fusion | flops 1536 | bytes 1032 | tf_op jit(solution)/shard_map/jit(_where)/select_n | solution.py:517
  9.7 0.0 copy-done
  9.7 0.0 copy-done.1
  9.7 0.0 copy-done.2
  9.7 0.0 copy-done.3
  9.7 0.0 copy-done.4
  9.7 0.0 copy-done.5
  9.7 61.5 %shard_map.131 = (f32[64,64]{1,0:T(8,128)S(1)}, bf16[256,128]{1,0:T(8,128)(2,1)S(1)}) custom-call(bf16[64,3072]{1,0:T(8,128)(2,1)S(1)} %bitcast.21, f32[64,64]{1,0:T(8,128)S(1)} %bitcast.25, bf16[256,128]{1,0:T(8,128)(2,1)S(1)} %bitcast.23, bf16[3072,256]{1,0:T(8,128)(2,1)S(1)} %maximum_maximum_fusion.wqkv, bf16[64,768]{1,0:T(8,128)(2,1)S(1)} %bitcast.22, ...), custom_call_target="tpu_custom_call" | custom-call | tf_op jit(solution)/shard_map/pallas_call | solution.py:522
  71.3 0.6 copy.21
  71.9 0.6 copy.22
  (17 shorter events, 0.1 us)
Async XLA Ops:
  3.6 1.2 %copy-start.6 = (f32[1,6,3072]{2,0,1:T(1,128)S(1)}, f32[1,6,3072]{2,0,1:T(1,128)}, u32[]{:S(2)}) copy-start(f32[1,6,3072]{2,0,1:T(1,128)} %param.17) | copy-start | bytes 221188
  3.7 2.5 %copy-start.7 = (s32[3,2,4,16]{3,2,1,0:T(4,128)S(1)}, s32[3,2,4,16]{3,2,1,0:T(4,128)}, u32[]{:S(2)}) copy-start(s32[3,2,4,16]{3,2,1,0:T(4,128)} %param.23) | copy-start | bytes 4612
  3.7 3.5 %copy-start.8 = (s32[2]{0:T(128)S(1)}, s32[2]{0:T(128)}, u32[]{:S(2)}) copy-start(s32[2]{0:T(128)} %param.21) | copy-start | bytes 28
  3.7 4.1 %copy-start.9 = (s32[4]{0:T(128)S(1)}, s32[4]{0:T(128)}, u32[]{:S(2)}) copy-start(s32[4]{0:T(128)} %param.22) | copy-start | bytes 52
  3.7 6.0 %copy-start = (bf16[1,4,16,3072]{3,2,1,0:T(8,128)(2,1)S(1)}, bf16[1,4,16,3072]{3,2,1,0:T(8,128)(2,1)}, u32[]{:S(2)}) copy-start(bf16[1,4,16,3072]{3,2,1,0:T(8,128)(2,1)} %param.12) | copy-start | bytes 1179652
  3.7 6.0 %copy-start.1 = (bf16[1,768,64]{1,2,0:T(8,128)(2,1)S(1)}, bf16[1,768,64]{1,2,0:T(8,128)(2,1)}, u32[]{:S(2)}) copy-start(bf16[1,768,64]{1,2,0:T(8,128)(2,1)} %param.16) | copy-start | bytes 294916
  3.7 6.0 %copy-start.2 = (bf16[1,1,1,256,128]{4,3,2,1,0:T(8,128)(2,1)S(1)}, bf16[1,1,1,256,128]{4,3,2,1,0:T(8,128)(2,1)}, u32[]{:S(2)}) copy-start(bf16[1,1,1,256,128]{4,3,2,1,0:T(8,128)(2,1)} %param.14) | copy-start | bytes 196612
  3.7 6.0 %copy-start.3 = (f32[1,4,16,64]{3,2,1,0:T(8,128)S(1)}, f32[1,4,16,64]{3,2,1,0:T(8,128)}, u32[]{:S(2)}) copy-start(f32[1,4,16,64]{3,2,1,0:T(8,128)} %param.13) | copy-start | bytes 49156
  3.7 6.0 %copy-start.4 = (f32[2,3072]{1,0:T(2,128)S(1)}, f32[2,3072]{1,0:T(2,128)}, u32[]{:S(2)}) copy-start(f32[2,3072]{1,0:T(2,128)} %omod.1) | copy-start | bytes 73732
  3.7 6.0 %copy-start.5 = (f32[1,3]{1,0:T(1,128)S(1)}, f32[1,3]{1,0:T(1,128)}, u32[]{:S(2)}) copy-start(f32[1,3]{1,0:T(1,128)} %coef.1) | copy-start | bytes 40

commit v3 on v2

--- a/solution.py
+++ b/solution.py
@@ -201,7 +201,7 @@
 
 
 def fused_kernel(
-    hid, lat, stale, wqkv, wout, mod, omod, proj, coef, cos_t, sin_t, bias,
+    hid, lat, stale, wqkv, wout, mod, omod, proj, coef, texts, videos, cos_t, sin_t,
     lat_out, cache_out,
     x_buf, mix, qkv_out, qkv_in, att_out, att_in, wo, mod0, fin, pred, pred_in,
     g_s, g_r, q_s, q_r, a_s, a_r, w_s, w_r, f_s, f_r, m_s, m_r, p_s, p_r, go,
@@ -249,11 +249,35 @@
             place(1, lax.rem(z + k, 4), c),
         )
 
-    def forward(layer, k):
-        return remote(
-            wo.at[layer, c], wo.at[layer, c], f_s.at[layer, k - 1], f_r.at[layer, k - 1],
-            place(1, z, lax.rem(c + k, 4)),
-        )
+    over_x = c + 1 - 2 * (c % 2)
+    over_y = lax.rem(c + 2, 4)
+    across = lax.rem(over_x + 2, 4)
+    steps = (
+        (c, 0, over_x), (c, 1, over_x), (c, 1, over_y), (c, 0, over_y),
+        (over_x, 0, over_y), (over_y, 1, over_x),
+    )
+    arrivals = ((over_x, 0), (over_x, 1), (over_y, 1), (over_y, 0), (across, 0), (across, 1))
+
+    def relay(blocks, sends, receives, j, section):
+        owner, half, target = steps[j]
+        part = blocks.at[owner, half * 32 : half * 32 + 32]
+        return remote(part, part, sends.at[j], receives.at[j], place(section, z, target))
+
+    def relay_landed(blocks, receives, j):
+        owner, half = arrivals[j]
+        landed(blocks.at[owner, half * 32 : half * 32 + 32], receives.at[j])
+
+    def forward(layer, j):
+        return relay(wo.at[layer], f_s.at[layer], f_r.at[layer], j, 1)
+
+    def forward_landed(layer, j):
+        relay_landed(wo.at[layer], f_r.at[layer], j)
+
+    def pass_on(layer):
+        forward_landed(layer, 0)
+        forward(layer, 4).start()
+        forward_landed(layer, 2)
+        forward(layer, 5).start()
 
     def shards_landed(layer):
         for zz in range(count):
@@ -266,8 +290,8 @@
                     landed(dst, w_r.at[layer, zz])
 
     def forwards_landed(layer):
-        for k in range(1, count):
-            landed(wo.at[layer, lax.rem(c + 4 - k, 4)], f_r.at[layer, k - 1])
+        for j in (1, 3, 4, 5):
+            forward_landed(layer, j)
 
     def text_mask(start, rows):
         i = lax.broadcasted_iota(jnp.int32, (rows, 1), 0) + start
@@ -307,8 +331,9 @@
         wo[1, c, :, own_cols] = wout[...]
         shards_landed(0)
         pl.semaphore_wait(go, 1)
-        for k in range(1, count):
-            forward(0, k).start()
+        for j in (0, 2, 1, 3):
+            forward(0, j).start()
+        pass_on(0)
         shards_landed(1)
         mod_copy.wait_recv()
         forwards_landed(0)
@@ -323,16 +348,16 @@
         mix[c, rows, :] = (normed * (1.0 + scale) + shift).astype(jnp.bfloat16)
         return carry
 
-    lax.fori_loop(0, 4, mix_rows, 0)
-
-    def gather(k):
-        return remote(
-            mix.at[c], mix.at[c], g_s.at[k - 1], g_r.at[k - 1], place(sec, z, lax.rem(c + k, 4))
-        )
-
-    for k in range(1, count):
-        gather(k).start()
-
+    def gather(j):
+        return relay(mix, g_s, g_r, j, sec)
+
+    lax.fori_loop(0, 2, mix_rows, 0)
+    gather(0).start()
+    lax.fori_loop(2, 4, mix_rows, 0)
+    for j in (2, 1, 3):
+        gather(j).start()
+
+    contract = (((1,), (1,)), ((), ()))
     lane = lax.broadcasted_iota(jnp.int32, (1, 128), 1)
     head = lane < HD
     low = (lane // 32) % 2 == 0
@@ -351,15 +376,23 @@
             qkv_out.at[s], qkv_in.at[:, z], q_s.at[s], q_r.at[z], place(sec, s, c)
         )
 
-    for k in range(count):
-        s = lax.rem(c + 4 - k, 4)
-        if k > 0:
-            landed(mix.at[s], g_r.at[k - 1])
-        projected = jnp.dot(mix[s], wqkv[...], preferred_element_type=jnp.float32)
+    for k, s in enumerate((c, over_x, over_y, across)):
+        if k == 1:
+            relay_landed(mix, g_r, 0)
+            gather(4).start()
+            relay_landed(mix, g_r, 2)
+            gather(5).start()
+            relay_landed(mix, g_r, 1)
+        if k == 2:
+            relay_landed(mix, g_r, 3)
+        if k == 3:
+            relay_landed(mix, g_r, 4)
+            relay_landed(mix, g_r, 5)
+        projected = lax.dot_general(mix[s], wqkv[...], contract, preferred_element_type=jnp.float32)
         cos_table = cos_t[s // 2]
         sin_table = sin_t[s // 2]
-        kv = prepare(projected[:, :128], cos_table, sin_table)
-        qq = prepare(projected[:, 128:], cos_table, sin_table)
+        kv = prepare(projected[:, HD:], cos_table, sin_table)
+        qq = prepare(projected[:, :128], cos_table, sin_table)
 
         qkv_out[s, :, :, :128] = kv
         qkv_out[s, :, :, 128:] = qq
@@ -376,24 +409,31 @@
 
     @pl.when(sec == 1)
     def _():
-        for k in range(1, count):
-            forward(1, k).start()
+        for j in (0, 2, 1, 3):
+            forward(1, j).start()
 
     qkv_in[:, z] = qkv_out[z]
     for k in range(1, count):
         zz = lax.rem(z + k, 4)
         landed(qkv_in.at[:, zz], q_r.at[zz])
+
+    @pl.when(sec == 1)
+    def _():
+        pass_on(1)
+
     fresh = qkv_in[:, :, :, :128].reshape(256, 128)
     query = qkv_in[:, :, :, 128:].reshape(256, 128)[:, :HD]
     cache_out[...] = fresh
     old = stale[...]
-    contract = (((1,), (1,)), ((), ()))
+    key_row = lax.broadcasted_iota(jnp.int32, (1, 256), 1)
+    limit = jnp.where(key_row < TEXT, texts[z], TEXT + videos[z // 2])
+    bias = jnp.where(key_row < limit, 0.0, -jnp.inf)
     fresh_scores = lax.dot_general(query, fresh[:, :HD], contract, preferred_element_type=jnp.float32)
     old_scores = lax.dot_general(query, old[:, :HD], contract, preferred_element_type=jnp.float32)
     query_patch = lax.broadcasted_iota(jnp.int32, (256, 256), 0) // 64
     key_patch = lax.broadcasted_iota(jnp.int32, (256, 256), 1) // 64
     is_fresh = key_patch <= query_patch
-    scores = jnp.where(is_fresh, fresh_scores, old_scores) * (HD ** -0.5) + bias[0:1, :]
+    scores = jnp.where(is_fresh, fresh_scores, old_scores) * (HD ** -0.5) + bias
     weights = jnp.exp(scores - jnp.max(scores, axis=1, keepdims=True))
     total = jnp.sum(weights, axis=1, keepdims=True)
     combined = jnp.dot(
@@ -442,7 +482,9 @@
             return carry
 
         lax.fori_loop(0, 4, last_rows, 0)
-        pred[...] = jnp.dot(fin[...], proj[...], preferred_element_type=jnp.float32)
+        pred[...] = lax.dot_general(
+            fin[...], proj[...], contract, preferred_element_type=jnp.float32
+        )
 
         @pl.when(c // 2 == 0)
         def _():
@@ -471,16 +513,18 @@
     def _():
         for k in range(1, count):
             shard_copy(1, k).wait_send()
-            forward(0, k).wait_send()
-            forward(1, k).wait_send()
             pred_copy(k).wait_send()
+        for j in range(6):
+            forward(0, j).wait_send()
+            forward(1, j).wait_send()
 
         @pl.when(c // 2 == 0)
         def _():
             pred_copy(0).wait_send()
 
+    for j in range(6):
+        gather(j).wait_send()
     for k in range(1, count):
-        gather(k).wait_send()
         qkv_copy(lax.rem(z + k, 4)).wait_send()
     for zz in range(count):
         stays = jnp.logical_and(sec == 1, jnp.logical_and(z == zz, c == z))
@@ -496,10 +540,7 @@
 ):
     z = lax.axis_index("seq")
     width = hidden_states.shape[3]
-    qkv = qkv_weight[0]
-    wqkv = jnp.concatenate(
-        [qkv[:, 1], qkv[:, 2], qkv[:, 0], jnp.zeros_like(qkv[:, 0])], axis=1
-    )
+    wqkv = qkv_weight[0].transpose(1, 2, 0).reshape(3 * HD, width)
     wout = out_weight[0].T
     rows = jnp.arange(64)
     row_place = (rows // 16) * 64 + z * 16 + rows % 16
@@ -510,11 +551,6 @@
     rest = jnp.zeros((2, 64, HD), jnp.float32)
     cos_t = jnp.concatenate([cos, cos, rest + 1.0], axis=-1)
     sin_t = jnp.concatenate([-sin, sin, rest], axis=-1)
-    row_ids = jnp.arange(256)
-    text_limit = lax.dynamic_index_in_dim(text_len, z, keepdims=False)
-    video_limit = lax.dynamic_index_in_dim(video_len, z // 2, keepdims=False)
-    live = jnp.where(row_ids < TEXT, row_ids < text_limit, row_ids - TEXT < video_limit)
-    bias = jnp.where(live, 0.0, -jnp.inf).astype(jnp.float32)[None]
     vmem = pl.BlockSpec(memory_space=pltpu.VMEM)
     smem = pl.BlockSpec(memory_space=pltpu.SMEM)
     dma = pltpu.SemaphoreType.DMA
@@ -525,7 +561,7 @@
             jax.ShapeDtypeStruct((64, 64), f32),
             jax.ShapeDtypeStruct((256, 128), bf16),
         ),
-        in_specs=[vmem] * 8 + [smem] + [vmem] * 3,
+        in_specs=[vmem] * 8 + [smem] * 3 + [vmem] * 2,
         out_specs=(vmem, vmem),
         scratch_shapes=[
             pltpu.VMEM((64, width), bf16),
@@ -539,8 +575,8 @@
             pltpu.VMEM((64, width), bf16),
             pltpu.VMEM((64, 64), f32),
             pltpu.VMEM((2, 64, 64), f32),
-            dma((3,)), dma((3,)), dma((4,)), dma((4,)), dma((4,)), dma((2, 4)),
-            dma((4,)), dma((2, 4)), dma((2, 3)), dma((2, 3)), dma, dma, dma((4,)), dma((2,)),
+            dma((6,)), dma((6,)), dma((4,)), dma((4,)), dma((4,)), dma((2, 4)),
+            dma((4,)), dma((2, 4)), dma((2, 6)), dma((2, 6)), dma, dma, dma((4,)), dma((2,)),
             pltpu.SemaphoreType.REGULAR,
         ],
         compiler_params=pltpu.CompilerParams(
@@ -548,7 +584,8 @@
         ),
     )(
         hidden_states.reshape(64, width), latent.reshape(64, 64), stale_cache[0, 0, 0], wqkv, wout,
-        modulation[0], out_modulation, proj_weight, solver_coef, cos_t, sin_t, bias,
+        modulation[0], out_modulation, proj_weight.T, solver_coef, text_len, video_len,
+        cos_t, sin_t,
     )
     return new_latent.reshape(latent.shape), new_cache.reshape(stale_cache.shape)
 

time: 72.7 us -> 66 us (0.908)
  Pallas kernels: 61.5 us -> 52.5 us
  local copies, waits for them, and re-layouts: 7.27 us -> 11 us
  other arithmetic: 2.82 us -> 1.21 us
    pallas_call x1, Pallas kernels: 61.5 us -> 52.5 us  [fused(): pl.pallas_call(fused_kernel, out_shape=(jax.ShapeDtypeStruct((64, 64), f3...]
    unnamed x25 -> x23, local copies, waits for them, and re-layouts: 5.46 us -> 10.6 us
    select_n x1 -> x0, other arithmetic: 1.3 us -> none  [fused(): bias = jnp.where(live, 0.0, -jnp.inf).astype(jnp.float32)[None]]
    dynamic_slice x2 -> x0, local copies, waits for them, and re-layouts: 1.17 us -> none  [the longest x1 0.59 us: fused(): video_limit = lax.dynamic_index_in_dim(video_len, z // 2, keepdims=False)]
    concatenate x1 -> x0, other arithmetic: 1.02 us -> none  [fused(): jnp.concatenate([qkv[:, 1], qkv[:, 2], qkv[:, 0], jnp.zeros_like(qkv[:, 0...]
where the time goes in v3:
time: 66 us; the launch traced here: 65.4 us
  Pallas kernels  52.5 us (80%)
  local copies, waits for them, and re-layouts  11 us (17%)
  other arithmetic  1.21 us (2%)
  between operations  0.71 us (1%)
    pallas_call x1, Pallas kernels, fused(): pl.pallas_call(fused_kernel, out_shape=(jax.ShapeDtypeStruct((64, 64), f3...  52.5 us
    unnamed x23, local copies, waits for them, and re-layouts  10.6 us

profile of v3, /device:TPU:0, one launch (start us, length us, event | category | flops | bytes accessed | tf_op | source)
XLA Modules:
  0.0 65.4 jit_solution(13405447679847930553)
XLA Ops:
  0.6 0.7 %convert_element_type.39 = f32[3,2,4,16]{3,2,1,0:T(4,128)S(1)} convert(s32[3,2,4,16]{3,2,1,0:T(4,128)} %param.23) | non-fusion elementwise | flops 384 | bytes 3072 | tf_op jit(solution)/shard_map/convert_element_type | solution.py:547
  1.3 0.1 mul.79
  1.4 0.1 mul.83
  1.5 0.1 mul.87
  1.7 0.4 fusion.10
  2.0 0.1 pad.2.clone
  2.1 0.1 pad.5.clone
  2.2 0.1 maximum_maximum_fusion
  2.3 0.9 %copy.16 = f32[1,6,3072]{2,1,0:T(8,128)S(1)} copy(f32[1,6,3072]{2,0,1:T(1,128)} %param.17) | data formatting | bytes 147456
  3.2 0.0 copy-start
  3.2 1.3 %copy-done = bf16[1,3072,3,64]{1,3,2,0:T(8,128)(2,1)S(1)} copy-done((bf16[1,3072,3,64]{1,3,2,0:T(8,128)(2,1)S(1)}, bf16[1,3072,3,64]{1,3,2,0:T(8,128)(2,1)}, u32[]{:S(2)}) %copy-start) | copy-done | bytes 1179672
  4.5 0.0 copy-start.1
  4.5 1.0 %copy-done.1 = bf16[1,4,16,3072]{3,2,1,0:T(8,128)(2,1)S(1)} copy-done((bf16[1,4,16,3072]{3,2,1,0:T(8,128)(2,1)S(1)}, bf16[1,4,16,3072]{3,2,1,0:T(8,128)(2,1)}, u32[]{:S(2)}) %copy-start.1) | copy-done | bytes 393240
  5.5 0.0 copy-start.2
  5.5 1.0 %copy-done.2 = bf16[3072,64]{0,1:T(8,128)(2,1)S(1)} copy-done((bf16[3072,64]{0,1:T(8,128)(2,1)S(1)}, bf16[3072,64]{0,1:T(8,128)(2,1)}, u32[]{:S(2)}) %copy-start.2) | copy-done | bytes 393240
  6.5 0.0 copy-start.3
  6.5 0.9 %copy-done.3 = bf16[1,768,64]{1,2,0:T(8,128)(2,1)S(1)} copy-done((bf16[1,768,64]{1,2,0:T(8,128)(2,1)S(1)}, bf16[1,768,64]{1,2,0:T(8,128)(2,1)}, u32[]{:S(2)}) %copy-start.3) | copy-done | bytes 98328
  7.4 0.0 copy-start.4
  7.4 0.8 %copy-done.4 = bf16[1,1,1,256,128]{4,3,2,1,0:T(8,128)(2,1)S(1)} copy-done((bf16[1,1,1,256,128]{4,3,2,1,0:T(8,128)(2,1)S(1)}, bf16[1,1,1,256,128]{4,3,2,1,0:T(8,128)(2,1)}, u32[]{:S(2)}) %copy-start.4) | copy-done | bytes 65560
  8.2 0.0 copy-start.5
  8.2 0.8 %copy-done.5 = f32[1,4,16,64]{3,2,1,0:T(8,128)S(1)} copy-done((f32[1,4,16,64]{3,2,1,0:T(8,128)S(1)}, f32[1,4,16,64]{3,2,1,0:T(8,128)}, u32[]{:S(2)}) %copy-start.5) | copy-done | bytes 16408
  9.0 0.0 copy-start.6
  9.0 0.7 %copy-done.6 = f32[2,3072]{1,0:T(2,128)S(1)} copy-done((f32[2,3072]{1,0:T(2,128)S(1)}, f32[2,3072]{1,0:T(2,128)}, u32[]{:S(2)}) %copy-start.6) | copy-done | bytes 24600
  9.7 0.0 copy-start.7
  9.7 0.7 copy-done.7
  10.4 0.0 copy-start.8
  10.4 0.7 copy-done.8
  11.0 0.0 copy-start.9
  11.0 0.7 copy-done.9
  11.7 52.5 %shard_map.131 = (f32[64,64]{1,0:T(8,128)S(1)}, bf16[256,128]{1,0:T(8,128)(2,1)S(1)}) custom-call(bf16[64,3072]{1,0:T(8,128)(2,1)S(1)} %bitcast.19, f32[64,64]{1,0:T(8,128)S(1)} %bitcast.24, bf16[256,128]{1,0:T(8,128)(2,1)S(1)} %bitcast.22, bf16[192,3072]{1,0:T(8,128)(2,1)S(1)} %bitcast.17, bf16[64,768]{1,0:T(8,128)(2,1)S(1)} %bitcast.21, ...), custom_call_target="tpu_custom_call" | custom-call | tf_op jit(solution)/shard_map/pallas_call | solution.py:558
  64.2 0.6 copy.19
  64.8 0.6 copy.20
  (8 shorter events, 0.0 us)
Async XLA Ops:
  3.2 1.3 %copy-start = (bf16[1,3072,3,64]{1,3,2,0:T(8,128)(2,1)S(1)}, bf16[1,3072,3,64]{1,3,2,0:T(8,128)(2,1)}, u32[]{:S(2)}) copy-start(bf16[1,3072,3,64]{1,3,2,0:T(8,128)(2,1)} %param.15) | copy-start | bytes 3538948
  4.5 1.0 %copy-start.1 = (bf16[1,4,16,3072]{3,2,1,0:T(8,128)(2,1)S(1)}, bf16[1,4,16,3072]{3,2,1,0:T(8,128)(2,1)}, u32[]{:S(2)}) copy-start(bf16[1,4,16,3072]{3,2,1,0:T(8,128)(2,1)} %param.12) | copy-start | bytes 1179652
  5.5 1.0 %copy-start.2 = (bf16[3072,64]{0,1:T(8,128)(2,1)S(1)}, bf16[3072,64]{0,1:T(8,128)(2,1)}, u32[]{:S(2)}) copy-start(bf16[3072,64]{0,1:T(8,128)(2,1)} %param.19) | copy-start | bytes 1179652
  6.5 0.9 %copy-start.3 = (bf16[1,768,64]{1,2,0:T(8,128)(2,1)S(1)}, bf16[1,768,64]{1,2,0:T(8,128)(2,1)}, u32[]{:S(2)}) copy-start(bf16[1,768,64]{1,2,0:T(8,128)(2,1)} %param.16) | copy-start | bytes 294916
  7.4 0.8 %copy-start.4 = (bf16[1,1,1,256,128]{4,3,2,1,0:T(8,128)(2,1)S(1)}, bf16[1,1,1,256,128]{4,3,2,1,0:T(8,128)(2,1)}, u32[]{:S(2)}) copy-start(bf16[1,1,1,256,128]{4,3,2,1,0:T(8,128)(2,1)} %param.14) | copy-start | bytes 196612
  8.2 0.8 %copy-start.5 = (f32[1,4,16,64]{3,2,1,0:T(8,128)S(1)}, f32[1,4,16,64]{3,2,1,0:T(8,128)}, u32[]{:S(2)}) copy-start(f32[1,4,16,64]{3,2,1,0:T(8,128)} %param.13) | copy-start | bytes 49156
  9.0 0.7 %copy-start.6 = (f32[2,3072]{1,0:T(2,128)S(1)}, f32[2,3072]{1,0:T(2,128)}, u32[]{:S(2)}) copy-start(f32[2,3072]{1,0:T(2,128)} %omod.1) | copy-start | bytes 73732
  9.7 0.7 %copy-start.7 = (f32[1,3]{1,0:T(1,128)S(1)}, f32[1,3]{1,0:T(1,128)}, u32[]{:S(2)}) copy-start(f32[1,3]{1,0:T(1,128)} %coef.1) | copy-start | bytes 40
  10.4 0.7 %copy-start.8 = (s32[4]{0:T(128)S(1)}, s32[4]{0:T(128)}, u32[]{:S(2)}) copy-start(s32[4]{0:T(128)} %texts.1) | copy-start | bytes 52
  11.0 0.7 %copy-start.9 = (s32[2]{0:T(128)S(1)}, s32[2]{0:T(128)}, u32[]{:S(2)}) copy-start(s32[2]{0:T(128)} %videos.1) | copy-start | bytes 28

commit v4 on v3

--- a/solution.py
+++ b/solution.py
@@ -201,15 +201,16 @@
 
 
 def fused_kernel(
-    hid, lat, stale, wqkv, wout, mod, omod, proj, coef, texts, videos, cos_t, sin_t,
+    hid_hbm, lat_hbm, stale_hbm, wqkv_hbm, wout_hbm, mod_hbm, omod_hbm, proj_hbm, coef, texts, videos, cos_t, sin_t,
     lat_out, cache_out,
-    x_buf, mix, qkv_out, qkv_in, att_out, att_in, wo, mod0, fin, pred, pred_in,
+    x_buf, lat, stale, wqkv, wout, mod, omod, proj, loads,
+    mix, qkv_out, qkv_in, att_out, att_in, wo, mod0, fin, pred, pred_in,
     g_s, g_r, q_s, q_r, a_s, a_r, w_s, w_r, f_s, f_r, m_s, m_r, p_s, p_r, go,
 ):
     sec = lax.axis_index("section")
     z = lax.axis_index("seq")
     c = lax.axis_index("cfg")
-    width = hid.shape[1]
+    width = hid_hbm.shape[1]
     shard = wout.shape[1]
     count = 4
 
@@ -238,8 +239,15 @@
         )
         return carry
 
+    sources = (hid_hbm, mod_hbm, wout_hbm, wqkv_hbm, stale_hbm, lat_hbm, omod_hbm, proj_hbm)
+    targets = (x_buf, mod, wout, wqkv, stale, lat, omod, proj)
+    local = [
+        pltpu.make_async_copy(source, target, loads.at[i])
+        for i, (source, target) in enumerate(zip(sources, targets))
+    ]
+    for copy in local:
+        copy.start()
     lax.fori_loop(1, everyone, greet, 0)
-    pl.semaphore_wait(barrier, everyone - 1)
 
     own_cols = pl.ds(pl.multiple_of(z * shard, 128), shard)
 
@@ -317,12 +325,35 @@
 
     mod_copy = remote(mod, mod0, m_s, m_r, place(1, z, c))
 
+    def mix_rows(p, carry):
+        rows = pl.ds(pl.multiple_of(p * 16, 16), 16)
+        text = text_mask(p * 16, 16)
+        normed = norm16(x_buf[rows, :])
+        scale = jnp.where(text, mod[4:5, :], mod[1:2, :])
+        shift = jnp.where(text, mod[3:4, :], mod[0:1, :])
+        mix[c, rows, :] = (normed * (1.0 + scale) + shift).astype(jnp.bfloat16)
+        return carry
+
+    def gather(j):
+        return relay(mix, g_s, g_r, j, sec)
+
+    local[0].wait()
+    local[1].wait()
+
     @pl.when(sec == 0)
     def _():
+        lax.fori_loop(0, 4, mix_rows, 0)
+
+    pl.semaphore_wait(barrier, everyone - 1)
+    local[2].wait()
+
+    @pl.when(sec == 0)
+    def _():
+        for j in (0, 2, 1, 3):
+            gather(j).start()
         mod_copy.start()
         for k in range(count):
             shard_copy(0, k).start()
-        x_buf[...] = hid[...]
 
     @pl.when(sec == 1)
     def _():
@@ -337,25 +368,15 @@
         shards_landed(1)
         mod_copy.wait_recv()
         forwards_landed(0)
-        out_projection(0, hid, mod0)
-
-    def mix_rows(p, carry):
-        rows = pl.ds(pl.multiple_of(p * 16, 16), 16)
-        text = text_mask(p * 16, 16)
-        normed = norm16(x_buf[rows, :])
-        scale = jnp.where(text, mod[4:5, :], mod[1:2, :])
-        shift = jnp.where(text, mod[3:4, :], mod[0:1, :])
-        mix[c, rows, :] = (normed * (1.0 + scale) + shift).astype(jnp.bfloat16)
-        return carry
-
-    def gather(j):
-        return relay(mix, g_s, g_r, j, sec)
-
-    lax.fori_loop(0, 2, mix_rows, 0)
-    gather(0).start()
-    lax.fori_loop(2, 4, mix_rows, 0)
-    for j in (2, 1, 3):
-        gather(j).start()
+        out_projection(0, x_buf, mod0)
+        lax.fori_loop(0, 2, mix_rows, 0)
+        gather(0).start()
+        lax.fori_loop(2, 4, mix_rows, 0)
+        for j in (2, 1, 3):
+            gather(j).start()
+
+    for copy in local[3:]:
+        copy.wait()
 
     contract = (((1,), (1,)), ((), ()))
     lane = lax.broadcasted_iota(jnp.int32, (1, 128), 1)
@@ -552,6 +573,7 @@
     cos_t = jnp.concatenate([cos, cos, rest + 1.0], axis=-1)
     sin_t = jnp.concatenate([-sin, sin, rest], axis=-1)
     vmem = pl.BlockSpec(memory_space=pltpu.VMEM)
+    far = pl.BlockSpec(memory_space=pl.ANY)
     smem = pl.BlockSpec(memory_space=pltpu.SMEM)
     dma = pltpu.SemaphoreType.DMA
     bf16, f32 = jnp.bfloat16, jnp.float32
@@ -561,10 +583,18 @@
             jax.ShapeDtypeStruct((64, 64), f32),
             jax.ShapeDtypeStruct((256, 128), bf16),
         ),
-        in_specs=[vmem] * 8 + [smem] * 3 + [vmem] * 2,
+        in_specs=[far] * 8 + [smem] * 3 + [vmem] * 2,
         out_specs=(vmem, vmem),
         scratch_shapes=[
             pltpu.VMEM((64, width), bf16),
+            pltpu.VMEM((64, 64), f32),
+            pltpu.VMEM((256, 128), bf16),
+            pltpu.VMEM((3 * HD, width), bf16),
+            pltpu.VMEM(wout.shape, bf16),
+            pltpu.VMEM((6, width), f32),
+            pltpu.VMEM((2, width), f32),
+            pltpu.VMEM((64, width), bf16),
+            dma((8,)),
             pltpu.VMEM((4, 64, width), bf16),
             pltpu.VMEM((4, 4, 16, 256), bf16),
             pltpu.VMEM((4, 4, 16, 256), bf16),
@@ -580,7 +610,7 @@
             pltpu.SemaphoreType.REGULAR,
         ],
         compiler_params=pltpu.CompilerParams(
-            collective_id=0, has_side_effects=True, vmem_limit_bytes=40 * 1024 * 1024
+            collective_id=0, has_side_effects=True, vmem_limit_bytes=64 * 1024 * 1024
         ),
     )(
         hidden_states.reshape(64, width), latent.reshape(64, 64), stale_cache[0, 0, 0], wqkv, wout,

time: 66 us -> 60.2 us (0.912)
  local copies, waits for them, and re-layouts: 11 us -> 4.79 us
    unnamed x23 -> x3, local copies, waits for them, and re-layouts: 10.6 us -> 4.38 us
where the time goes in v4:
time: 60.2 us; the launch traced here: 59.8 us
  Pallas kernels  52.5 us (87%)
  local copies, waits for them, and re-layouts  4.79 us (8%)
  other arithmetic  1.85 us (3%)
  between operations  0.68 us (1%)
    pallas_call x1, Pallas kernels, fused(): pl.pallas_call(fused_kernel, out_shape=(jax.ShapeDtypeStruct((64, 64), f3...  52.5 us
    unnamed x3, local copies, waits for them, and re-layouts  4.38 us

profile of v4, /device:TPU:0, one launch (start us, length us, event | category | flops | bytes accessed | tf_op | source)
XLA Modules:
  0.0 59.8 jit_solution(4307957224480146879)
XLA Ops:
  0.6 0.7 %convert_element_type.39 = f32[3,2,4,16]{3,2,1,0:T(4,128)S(1)} convert(s32[3,2,4,16]{3,2,1,0:T(4,128)} %param.23) | non-fusion elementwise | flops 384 | bytes 3072 | tf_op jit(solution)/shard_map/convert_element_type | solution.py:568
  1.3 0.1 mul.79
  1.4 0.1 mul.83
  1.5 0.1 mul.87
  1.7 0.4 fusion.10
  2.0 0.1 pad.2.clone
  2.1 0.1 pad.5.clone
  2.2 0.7 %maximum_maximum_fusion = (f32[2,64,128]{2,1,0:T(8,128)}, f32[2,64,128]{2,1,0:T(8,128)}) fusion(f32[2,64,32]{2,1,0:T(8,128)S(1)} %get-tuple-element.11, f32[128]{0:T(128)S(1)} %pad.5.clone, f32[128]{0:T(128)S(1)} %pad.2.clone, f32[2,64,32]{2,1,0:T(8,128)S(1)} %get-tuple-element.10, f32[2,64,32]{2,1,0:T(8,128)S(1)} %get-tuple-element.9), kind=kLoop, calls=%fused_computation.1 | loop fusion | flops 65536 | bytes 181248 | tf_op jit(solution)/shard_map/concatenate | solution.py:573
  2.9 1.5 %copy.16 = f32[1,6,3072]{2,1,0:T(8,128)} copy(f32[1,6,3072]{2,0,1:T(1,128)} %param.17) | data formatting | bytes 147456
  4.5 52.5 %shard_map.131 = (f32[64,64]{1,0:T(8,128)}, bf16[256,128]{1,0:T(8,128)(2,1)}) custom-call(bf16[64,3072]{1,0:T(8,128)(2,1)} %bitcast.19, f32[64,64]{1,0:T(8,128)} %bitcast.24, bf16[256,128]{1,0:T(8,128)(2,1)} %bitcast.22, bf16[192,3072]{1,0:T(8,128)(2,1)} %bitcast.17, bf16[64,768]{1,0:T(8,128)(2,1)} %bitcast.21, f32[6,3072]{1,0:T(8,128)} %bitcast.18, ...), custom_call_target="tpu_custom_call" | custom-call | tf_op jit(solution)/shard_map/pallas_call | solution.py:580
  57.0 1.4 %copy.19 = f32[1,4,16,64]{3,2,1,0:T(8,128)} copy(f32[1,4,16,64]{3,2,1,0:T(8,128)} %bitcast.25) | data formatting | bytes 32768
  58.4 1.5 %copy.20 = bf16[1,1,1,256,128]{4,3,2,1,0:T(8,128)(2,1)} copy(bf16[1,1,1,256,128]{4,3,2,1,0:T(8,128)(2,1)} %bitcast.23) | data formatting | bytes 131072
  (8 shorter events, 0.0 us)
